TPU v7x, 512 devices: a whole 4x8x8 slice. The times are simulated.
512 devices in a mesh: dp: 8 (over y_hi, x), fsdp: 64 (over y_lo, z, core).
Axes of the slice: x: 4, y: 8 (y_hi: 2, y_lo: 4; y = y_hi * 4 + y_lo), z: 8, core: 2. Of those that a mesh axis runs over, the one named last changes fastest.
Arguments:
- activations: bfloat16 [131072, 8192], P(('dp', 'fsdp')), may hold values from -24 to 24
- value_weight: bfloat16 [8192, 128], P('fsdp'), may hold values from -0.0625 to 0.0625
- sensitivity: bfloat16 [131072, 128], P(('dp', 'fsdp')), may hold values from -6 to 6
- policy_logp: float32 [131072], P(('dp', 'fsdp')), may hold values from -0.7 to -0.3
- reference_logp: float32 [131072], P(('dp', 'fsdp')), may hold values from -0.7 to -0.3
- prompt_len: int32 [16], replicated, may hold values from 512 to 2047
Outputs:
- projected: bfloat16 [131072, 128], P(('dp', 'fsdp'))
- weight_grad: float32 [8192, 128], P('fsdp')
- margins: float32 [16], replicated
- loss: float32 [], replicated
Inputs may be any that keep to these rules, and one draw needn't show every extreme that they name: `prompt_len`: shared by the chosen and the rejected sequence of the pair.
All inputs are finite; a program needn't handle non-finite values.
Results may differ from a plain program's by a relative error of at most 0.0029.
Values may be sent and summed in bfloat16 or wider, within the bound.
No kernel may reach another device: no remote copies, remote signals or barrier semaphores. Data moves between devices by JAX's collectives and lax.ppermute only.
A program may use at most 64 MiB of HBM per device.

v0:
```python
import jax
import jax.numpy as jnp
from jax import lax
from jax.sharding import PartitionSpec as P

SEQ = 4096


BETA = 0.1


def body(activations, value_weight, sensitivity, policy_logp, reference_logp, prompt_len):
    row_count = activations.shape[0]
    fsdp_count = lax.axis_size("fsdp")
    first_row = (lax.axis_index("dp") * fsdp_count + lax.axis_index("fsdp")) * row_count
    columns = activations
    projected = jnp.dot(
        columns,
        lax.all_gather(value_weight, "fsdp", axis=0, tiled=True),
        preferred_element_type=jnp.float32,
    ).astype(jnp.bfloat16)
    pair_count = prompt_len.shape[0]
    seq_count = 2 * pair_count
    position = first_row + jnp.arange(row_count, dtype=jnp.int32)
    sequence = position // SEQ
    offset = position % SEQ
    pair_onehot = sequence[:, None] // 2 == jnp.arange(pair_count, dtype=jnp.int32)[None, :]
    prompt_here = jnp.sum(jnp.where(pair_onehot, prompt_len[None, :], 0), axis=1)
    mask = offset >= prompt_here
    difference = jnp.where(mask, policy_logp - reference_logp, jnp.float32(0.0))
    seq_onehot = (sequence[:, None] == jnp.arange(seq_count, dtype=jnp.int32)[None, :]).astype(
        jnp.float32
    )
    partial_totals = jnp.sum(seq_onehot * difference[:, None], axis=0)
    group_totals = lax.psum(partial_totals, "fsdp")
    totals = lax.psum(group_totals, "dp")
    margins = BETA * (totals[0::2] - totals[1::2])
    loss = jnp.mean(jax.nn.softplus(-margins))
    pair_scale = -BETA * jax.nn.sigmoid(-margins) / pair_count
    seq_scale = jnp.stack([pair_scale, -pair_scale], axis=1).reshape(seq_count)
    token_scale = jnp.where(
        mask, jnp.sum(seq_onehot * seq_scale[None, :], axis=1), jnp.float32(0.0)
    )
    cotangent = (token_scale[:, None] * sensitivity.astype(jnp.float32)).astype(jnp.bfloat16)
    columns = activations
    owned = lax.psum_scatter(
        lax.dot_general(
            columns, cotangent, (((0,), (0,)), ((), ())), preferred_element_type=jnp.float32
        ),
        "fsdp",
        scatter_dimension=0,
        tiled=True,
    )
    weight_grad = lax.psum(owned, "dp")
    return (projected, weight_grad, margins, loss)


def solution(mesh):
    return jax.shard_map(
        body,
        mesh=mesh,
        in_specs=(
            P(("dp", "fsdp"), None),
            P("fsdp", None),
            P(("dp", "fsdp"), None),
            P(("dp", "fsdp")),
            P(("dp", "fsdp")),
            P(),
        ),
        out_specs=(P(("dp", "fsdp"), None), P("fsdp", None), P(), P()),
        check_vma=False,
    )
```

profile of v0, /device:TPU:8, one launch (start us, length us, event | category | flops | bytes accessed | tf_op | source)
XLA Modules:
  0.0 700.9 jit_solution(13926234858815961203)
XLA Ops:
  7.2 0.0 reduce-scatter.2.cloned.1.call-start
  7.2 0.7 select_reduce_fusion.2
  8.0 0.7 subtract_select_fusion
  8.7 0.1 select_reduce_fusion.1
  8.8 113.0 %psum.21 = f32[32]{0:T(128)S(1)} all-reduce(f32[32]{0:T(128)S(1)} %select_reduce_fusion.1), channel_id=1, replica_groups=mesh['dp'=8,'fsdp'=64] {'fsdp'}, use_global_device_ids=true, to_apply=%region_2.3 | all-reduce | flops 32 | bytes 256 | tf_op jit(solution)/shard_map/psum | solution.py:35
  121.8 31.8 %psum.22 = f32[32]{0:T(128)S(1)} all-reduce(f32[32]{0:T(128)S(1)} %psum.21), channel_id=1, replica_groups=mesh['dp'=8,'fsdp'=64] {'dp'}, use_global_device_ids=true, to_apply=%region_3.4 | all-reduce | flops 32 | bytes 256 | tf_op jit(solution)/shard_map/psum | solution.py:36
  153.6 0.1 slice.6
  153.7 0.1 slice.7
  153.8 0.6 fusion.3
  154.4 0.0 copy-start
  154.5 0.1 copy.14
  154.6 0.1 mul.41
  154.7 0.1 select_reduce_fusion
  154.8 5.0 convolution_bitcast_fusion
  159.7 0.0 copy-done
  159.8 0.0 reduce-scatter.2.cloned.1.call-update
  159.8 0.0 all-gather.2.cloned.1.call-start
  159.8 0.7 all-gather.2.cloned.1.call-update
  160.5 0.0 all-reduce.2.cloned.1.call-start
  161.2 264.9 %reduce-scatter.2.cloned.1.call-done = f32[128,128]{0,1:T(8,128)} async-done(((f32[8192,128]{0,1:T(8,128)}), f32[128,128]{0,1:T(8,128)}) %reduce-scatter.2.cloned.1.call-update) | async-done | bytes 65552 | tf_op jit(solution)/shard_map/reduce_scatter | solution.py:46
  426.1 0.0 all-reduce.2.cloned.1.call-update
  426.1 153.3 %all-gather.2.cloned.1.call-done = bf16[8192,128]{1,0:T(8,128)(2,1)} async-done(((bf16[128,128]{1,0:T(8,128)(2,1)}), bf16[8192,128]{1,0:T(8,128)(2,1)}) %all-gather.2.cloned.1.call-update) | async-done | bytes 2097168 | tf_op jit(solution)/shard_map/all_gather | solution.py:19
  579.4 4.7 convolution_convert_fusion
  584.2 107.5 %all-reduce.2.cloned.1.call-done = f32[128,128]{0,1:T(8,128)} async-done(((f32[128,128]{0,1:T(8,128)}), f32[128,128]{0,1:T(8,128)}) %all-reduce.2.cloned.1.call-update) | async-done | bytes 65552 | tf_op jit(solution)/shard_map/psum | solution.py:54
  691.7 1.6 copy.15
  (4 shorter events, 0.0 us)
Async XLA Ops:
  7.2 418.9 %reduce-scatter.2.cloned.1.call-start = ((), (), s32[]{:S(2)}) async-start(), calls=%async_computation.2 | async-start | bytes 4259840 | tf_op jit(solution)/shard_map/reduce_scatter | solution.py:46
  154.4 5.3 copy-start
  159.8 419.7 %all-gather.2.cloned.1.call-start = ((), (), s32[]{:S(2)}) async-start(), calls=%async_computation.1 | async-start | bytes 2129920 | tf_op jit(solution)/shard_map/all_gather | solution.py:19
  160.5 531.1 %all-reduce.2.cloned.1.call-start = ((), (), s32[]{:S(2)}) async-start(), calls=%async_computation.3 | async-start | bytes 131072 | tf_op jit(solution)/shard_map/psum | solution.py:54
Sparse Core Ops, SparseCore 0:
  159.9 266.1 reduce-scatter.1
  428.5 150.9 all-gather.1
  582.6 109.0 all-reduce.1
where the time goes:
time: 701 us
  waiting for transfers between devices  526 us (75%)
  blocking collectives  145 us (21%)
  between operations  15.5 us (2%)
  matrix products  9.73 us (1%)
    reduce_scatter x1, waiting for transfers between devices, body(): lax.psum_scatter(lax.dot_general(columns, cotangent, (((0,), (0,)), ((),...  265 us
    all_gather x1, waiting for transfers between devices, body(): lax.all_gather(value_weight, 'fsdp', axis=0, tiled=True)  153 us
    psum x1, blocking collectives, body(): group_totals = lax.psum(partial_totals, 'fsdp')  113 us
    psum x1, waiting for transfers between devices, body(): weight_grad = lax.psum(owned, 'dp')  107 us
    psum x1, blocking collectives, body(): totals = lax.psum(group_totals, 'dp')  31.8 us
  transfers between devices with their start and end apart: 3, of which 3 were waited for; matrix products, arithmetic and copies ran while one was open for 1% of the time, Pallas kernels for 0%

commit v1 on v0

v1 whole, which is shorter than its diff:
```python
import jax
import jax.numpy as jnp
from jax import lax
from jax.sharding import Mesh, PartitionSpec as P

SEQ = 4096
BETA = 0.1
HEAD = 128
EXTRA = 16

SIZES = (("yh", 2), ("x", 4), ("yp", 2), ("yq", 2), ("z", 8), ("c", 2))
NAMES = tuple(name for name, _ in SIZES)
DP = ("yh", "x")
FSDP = ("yp", "yq", "z", "c")
SWAP = ((0, 1), (1, 0))


def pieces(value):
    high = lax.reduce_precision(value, 8, 7)
    rest = value - high
    middle = lax.reduce_precision(rest, 8, 7)
    low = lax.reduce_precision(rest - middle, 8, 7)
    return jnp.stack([high, middle, low]).astype(jnp.bfloat16)


def packed(value):
    rows = jnp.concatenate([pieces(value), jnp.zeros((EXTRA - 3,), jnp.bfloat16)])
    return jnp.broadcast_to(rows[:, None], (EXTRA, HEAD))


def unpacked(rows):
    return jnp.sum(rows[..., :3, 0].astype(jnp.float32), axis=-1)


def pick(index, first, second):
    return jnp.where(index == 0, first, second)


def body(activations, value_weight, sensitivity, policy_logp, reference_logp, prompt_len):
    row_count, width = activations.shape
    pair_count = prompt_len.shape[0]
    yh, x, yp, yq, z, c = (lax.axis_index(name) for name in NAMES)
    xs, zs = 4, 8
    blocks = width // HEAD // 2

    pair = (yh * xs + x) * 2 + yp
    prompt_here = lax.dynamic_index_in_dim(prompt_len, pair, keepdims=False)
    ramp = jnp.arange(row_count, dtype=jnp.int32)
    mask_own = (z * 2 + c) * row_count + ramp >= prompt_here
    mask_other = (z * 2 + 1 - c) * row_count + ramp >= prompt_here
    part = jnp.sum(jnp.where(mask_own, policy_logp - reference_logp, jnp.float32(0.0)))

    sens_and_part = jnp.concatenate([sensitivity, packed(part)])
    other = lax.ppermute(sens_and_part, "c", SWAP)
    sens_other = other[:row_count]
    part_chip = part + unpacked(other[row_count:])
    by_core = activations.reshape(row_count, blocks, 2, HEAD)
    even, odd = by_core[:, :, 0], by_core[:, :, 1]
    act_own = pick(c, even, odd).reshape(row_count, width // 2)
    act_other = lax.ppermute(pick(c, odd, even).reshape(row_count, width // 2), "c", SWAP)

    block = jnp.concatenate([value_weight, packed(part_chip)])
    height = block.shape[0]
    near = lax.all_to_all(
        jnp.broadcast_to(block[None], (2 * zs, height, HEAD)).reshape(-1, HEAD), ("yq", "z"), 0, 0, tiled=True
    ).reshape(2 * zs, height, HEAD)
    totals = jnp.sum(unpacked(near[:, HEAD:]).reshape(2, zs), axis=1)
    margin = BETA * (totals[0] - totals[1])

    outside = [(y, (y + 1) % 8 if y % 2 else (y - 1) % 8) for y in range(8)]
    far = lax.ppermute(near, ("yh", "yp", "yq"), outside)
    far_totals = jnp.sum(unpacked(far[:, HEAD:]).reshape(2, zs), axis=1)
    far_margin = BETA * (far_totals[0] - far_totals[1])

    pair_scale = -BETA * jax.nn.sigmoid(-margin) / pair_count
    scale = pick(yq, pair_scale, -pair_scale)

    def cotangent(mask, sens):
        token_scale = jnp.where(mask, scale, jnp.float32(0.0))
        return (token_scale[:, None] * sens.astype(jnp.float32)).astype(jnp.bfloat16)

    def term(act, mask, sens):
        return lax.dot_general(
            act, cotangent(mask, sens), (((0,), (0,)), ((), ())), preferred_element_type=jnp.float32
        )

    grad = term(act_own, mask_own, sensitivity) + term(act_other, mask_other, sens_other)
    rows = HEAD // xs
    grad = grad.reshape(blocks, xs, rows, HEAD)

    def chunk(index):
        return lax.dynamic_index_in_dim(grad, index % xs, axis=1, keepdims=False)

    reduced = chunk(x)
    for step in (2, 1, 3):
        sent = lax.ppermute(
            chunk(x + step).astype(jnp.bfloat16), "x", [(i, (i + step) % xs) for i in range(xs)]
        )
        reduced = reduced + sent.astype(jnp.float32)
    terms = lax.all_to_all(
        reduced.astype(jnp.bfloat16).reshape(blocks * rows, HEAD), ("yp", "yq", "z"), 0, 0, tiled=True
    ).reshape(blocks, rows, HEAD)
    reduced = jnp.sum(terms.astype(jnp.float32), axis=0)

    near_w, far_w = near[:, :HEAD].reshape(-1, HEAD), far[:, :HEAD].reshape(-1, HEAD)
    weight = jnp.concatenate([pick(yp, near_w, far_w), pick(yp, far_w, near_w)])
    half_own = jnp.dot(act_own, weight, preferred_element_type=jnp.float32)
    half_other = jnp.dot(act_other, weight, preferred_element_type=jnp.float32)
    projected = (half_own + lax.ppermute(half_other, "c", SWAP)).astype(jnp.bfloat16)

    tail = jnp.concatenate([
        jnp.broadcast_to(margin, (1, HEAD)),
        jnp.broadcast_to(far_margin, (1, HEAD)),
        jnp.zeros((6, HEAD), jnp.float32),
    ])
    share = jnp.concatenate([reduced, tail])
    high = share.shape[0]
    shares = lax.all_to_all(
        jnp.broadcast_to(share[None], (2 * xs, high, HEAD)).reshape(-1, HEAD), DP, 0, 0, tiled=True
    ).reshape(2, xs, high, HEAD)
    weight_grad = (shares[0, :, :rows] + shares[1, :, :rows]).reshape(HEAD, HEAD)
    near_m = shares[:, :, rows, 0]
    far_m = shares[:, :, rows + 1, 0]
    far_m = jnp.where(yp == yq, far_m[::-1], far_m)
    margins = jnp.stack([pick(yp, near_m, far_m), pick(yp, far_m, near_m)], axis=-1).reshape(pair_count)
    loss = jnp.mean(jax.nn.softplus(-margins))
    return projected, weight_grad, margins, loss


def solution(mesh):
    devices = mesh.devices.reshape(tuple(size for _, size in SIZES))
    return jax.shard_map(
        body,
        mesh=Mesh(devices, NAMES),
        in_specs=(
            P(DP + FSDP, None),
            P(FSDP, None),
            P(DP + FSDP, None),
            P(DP + FSDP),
            P(DP + FSDP),
            P(),
        ),
        out_specs=(P(DP + FSDP, None), P(FSDP, None), P(), P()),
        check_vma=False,
    )
```

time: 701 us -> 136 us (0.19)
  waiting for transfers between devices: 526 us -> 31.9 us
  blocking collectives: 145 us -> 0 us
  starting transfers between devices: 0.12 us -> 47.2 us
  local copies, waits for them, and re-layouts: 1.96 us -> 15.8 us
  other arithmetic: 2.33 us -> 15.1 us
    reduce_scatter x1 -> x0, waiting for transfers between devices: 265 us -> none  [body(): lax.psum_scatter(lax.dot_general(columns, cotangent, (((0,), (0,)), ((),...]
    all_gather x1 -> x0, waiting for transfers between devices: 153 us -> none  [body(): lax.all_gather(value_weight, 'fsdp', axis=0, tiled=True)]
    psum x2 -> x0, blocking collectives: 145 us -> none  [the longest x1 113 us: body(): group_totals = lax.psum(partial_totals, 'fsdp')]
    psum x1 -> x0, waiting for transfers between devices: 107 us -> none  [body(): weight_grad = lax.psum(owned, 'dp')]
    all_to_all x0 -> x3, waiting for transfers between devices: none -> 28.8 us  [the longest x1 16.4 us: body(): lax.all_to_all(jnp.broadcast_to(block[None], (2 * zs, height, HEAD)).resh...]
    all_to_all x0 -> x3, starting transfers between devices: none -> 26.7 us  [the longest x1 11.8 us: body(): lax.all_to_all(jnp.broadcast_to(block[None], (2 * zs, height, HEAD)).resh...]
    ppermute x0 -> x7, starting transfers between devices: none -> 20.5 us  [the longest x3 10.8 us: body(): lax.ppermute(chunk(x + step).astype(jnp.bfloat16), 'x', [(i, (i + step) %...]
  transfers between devices with their start and end apart: 3 -> 10, of which waited for: 3 -> 4; matrix products, arithmetic and copies ran while one was open for 1% -> 21% of each run, Pallas kernels for 0% -> 0%
where the time goes in v1:
time: 136 us; the launch traced here: 134 us
  starting transfers between devices  47.2 us (35%)
  waiting for transfers between devices  31.9 us (23%)
  between operations  16.2 us (12%)
  local copies, waits for them, and re-layouts  15.8 us (12%)
  other arithmetic  15.1 us (11%)
  matrix products  8.09 us (6%)
    all_to_all x1, waiting for transfers between devices, body(): lax.all_to_all(jnp.broadcast_to(block[None], (2 * zs, height, HEAD)).resh...  16.4 us
    all_to_all x1, starting transfers between devices, body(): lax.all_to_all(jnp.broadcast_to(block[None], (2 * zs, height, HEAD)).resh...  11.8 us
    ppermute x3, starting transfers between devices, body(): lax.ppermute(chunk(x + step).astype(jnp.bfloat16), 'x', [(i, (i + step) %...  10.8 us
    all_to_all x1, starting transfers between devices, body(): lax.all_to_all(reduced.astype(jnp.bfloat16).reshape(blocks * rows, HEAD),...  10.7 us
    unnamed x17, local copies, waits for them, and re-layouts  8.57 us
    all_to_all x1, waiting for transfers between devices, body(): lax.all_to_all(jnp.broadcast_to(share[None], (2 * xs, high, HEAD)).reshap...  8.23 us
    select_n x2, other arithmetic, pick(): return jnp.where(index == 0, first, second)  4.96 us
    all_to_all x1, waiting for transfers between devices, body(): lax.all_to_all(reduced.astype(jnp.bfloat16).reshape(blocks * rows, HEAD),...  4.21 us
  transfers between devices with their start and end apart: 10, of which 4 were waited for; matrix products, arithmetic and copies ran while one was open for 21% of the time, Pallas kernels for 0%

profile of v1, /device:TPU:8, one launch (start us, length us, event | category | flops | bytes accessed | tf_op | source)
XLA Modules:
  0.0 134.3 jit_solution(1012110237335137395)
XLA Ops:
  0.6 1.2 dynamic_slice.17
  1.9 1.9 %select_reduce_fusion = f32[]{:T(128)} fusion(f32[256]{0:T(256)} %param.9, f32[256]{0:T(256)} %param.10, s32[]{:T(128)} %bitcast.2, s32[]{:T(128)S(6)} %mul.45), kind=kLoop, calls=%fused_computation.42 | loop fusion | flops 1279 | bytes 2060 | tf_op jit(solution)/shard_map/reduce_sum | solution.py:51
  9.3 0.7 fusion.20
  10.0 0.9 pad_maximum_fusion.7
  10.9 1.9 %collective-permute-start = (bf16[272,128]{1,0:T(8,128)(2,1)S(1)}, bf16[272,128]{1,0:T(8,128)(2,1)S(1)}, u32[]{:S(2)}, u32[]{:S(2)}) collective-permute-start(bf16[272,128]{1,0:T(8,128)(2,1)S(1)} %pad_maximum_fusion.7), channel_id=1, source_target_pairs={{0,1},{1,0},{2,3},{3,2},{4,5},{5,4},{6,7},{7,6},{8,9},{9,8},{10,11... | collective-permute-start | bytes 208904 | tf_op jit(solution)/shard_map/ppermute | solution.py:54
  12.9 6.4 %copy.37 = bf16[256,8192]{0,1:T(8,128)(2,1)} copy(bf16[256,8192]{1,0:T(8,128)(2,1)} %param.6) | data formatting | bytes 8388608 | tf_op args[0]
  19.3 3.8 %broadcast_select_fusion.1 = (bf16[256,32,1,128]{0,3,2,1:T(8,128)(2,1)S(1)}, bf16[256,32,1,128]{0,3,2,1:T(8,128)(2,1)}) fusion(pred[]{:T(512)S(6)} %eq.21, bf16[256,32,2,128]{0,3,2,1:T(8,128)(2,1)} %bitcast.49), kind=kLoop, calls=%fused_computation.2 | loop fusion | flops 2097152 | bytes 8388609 | tf_op jit(solution)/shard_map/jit(_where)/select_n | solution.py:36
  23.1 2.5 %collective-permute-start.2 = (bf16[256,4096]{0,1:T(8,128)(2,1)}, bf16[256,4096]{0,1:T(8,128)(2,1)}, u32[]{:S(2)}, u32[]{:S(2)}) collective-permute-start(bf16[256,4096]{0,1:T(8,128)(2,1)} %bitcast.11), channel_id=1, source_target_pairs={{0,1},{1,0},{2,3},{3,2},{4,5},{5,4},{6,7},{7,6},{8,9},{9,8},{10,11... | collective-permute-start | bytes 6291464 | tf_op jit(solution)/shard_map/ppermute | solution.py:60
  31.7 0.7 select_maximum_fusion
  32.5 0.9 broadcast_in_dim.50
  33.4 11.8 %all-to-all-start = ((bf16[16,144,128]{2,1,0:T(8,128)(2,1)}), bf16[16,144,128]{2,1,0:T(8,128)(2,1)S(1)}, u32[]{:S(2)}, u32[]{:S(2)}) async-start(bf16[16,144,128]{2,1,0:T(8,128)(2,1)} %broadcast_in_dim.50), calls=%async_computation | async-start | bytes 1179648 | tf_op jit(solution)/shard_map/all_to_all | solution.py:64
  45.2 16.4 %all-to-all-done = bf16[16,144,128]{2,1,0:T(8,128)(2,1)S(1)} async-done(((bf16[16,144,128]{2,1,0:T(8,128)(2,1)}), bf16[16,144,128]{2,1,0:T(8,128)(2,1)S(1)}, u32[]{:S(2)}, u32[]{:S(2)}) %all-to-all-start) | async-done | bytes 589856 | tf_op jit(solution)/shard_map/all_to_all | solution.py:64
  63.9 3.3 %collective-permute-start.1 = (bf16[16,144,128]{2,1,0:T(8,128)(2,1)S(1)}, bf16[16,144,128]{2,1,0:T(8,128)(2,1)S(1)}, u32[]{:S(2)}, u32[]{:S(2)}) collective-permute-start(bf16[16,144,128]{2,1,0:T(8,128)(2,1)S(1)} %all-to-all-done), channel_id=1, source_target_pairs={{0,304},{16,32},{32,16},{48,256},{256,48},{272,288},{288,272},{304... | collective-permute-start | bytes 1769480 | tf_op jit(solution)/shard_map/ppermute | solution.py:71
  67.9 0.8 fusion.10
  68.7 2.4 %convolution_add_fusion = f32[4096,128]{1,0:T(8,128)S(1)} fusion(f32[4096,128]{1,0:T(8,128)S(1)} %fusion.10, bf16[256,4096]{0,1:T(8,128)(2,1)} %collective-permute-done.2, bf16[272,128]{1,0:T(8,128)(2,1)S(1)} %collective-permute-done, f32[256]{0:T(256)S(1)} %get-tuple-element.21), kind=kOutput, calls=%fused_computation | convolution fusion | flops 269058048 | bytes 6358016 | tf_op jit(solution)/shard_map/dot_general | solution.py:83
  71.1 1.3 copy-done
  72.4 1.0 fusion.8
  73.4 4.7 %collective-permute-start.6 = (bf16[32,32,128]{2,1,0:T(8,128)(2,1)}, bf16[32,32,128]{2,1,0:T(8,128)(2,1)}, u32[]{:S(2)}, u32[]{:S(2)}) collective-permute-start(bf16[32,32,128]{2,1,0:T(8,128)(2,1)} %get-tuple-element.9), channel_id=1, source_target_pairs={{0,192},{64,0},{128,64},{192,128},{1,193},{65,1},{129,65},{193,129... | collective-permute-start | bytes 786440 | tf_op jit(solution)/shard_map/ppermute | solution.py:96
  78.0 1.9 %collective-permute-start.5 = (bf16[32,32,128]{2,1,0:T(8,128)(2,1)}, bf16[32,32,128]{2,1,0:T(8,128)(2,1)}, u32[]{:S(2)}, u32[]{:S(2)}) collective-permute-start(bf16[32,32,128]{2,1,0:T(8,128)(2,1)} %get-tuple-element.10), channel_id=1, source_target_pairs={{0,64},{64,128},{128,192},{192,0},{1,65},{65,129},{129,193},{193,1... | collective-permute-start | bytes 786440 | tf_op jit(solution)/shard_map/ppermute | solution.py:96
  80.0 4.2 %collective-permute-start.4 = (bf16[32,32,128]{2,1,0:T(8,128)(2,1)S(1)}, bf16[32,32,128]{2,1,0:T(8,128)(2,1)}, u32[]{:S(2)}, u32[]{:S(2)}) collective-permute-start(bf16[32,32,128]{2,1,0:T(8,128)(2,1)S(1)} %get-tuple-element.8), channel_id=1, source_target_pairs={{0,128},{64,192},{128,0},{192,64},{1,129},{65,193},{129,1},{193,65... | collective-permute-start | bytes 786440 | tf_op jit(solution)/shard_map/ppermute | solution.py:96
  85.4 0.7 copy.46
  86.1 0.7 convert_reduce_fusion.2
  89.0 3.1 %collective-permute-done.5 = bf16[32,32,128]{2,1,0:T(8,128)(2,1)} collective-permute-done((bf16[32,32,128]{2,1,0:T(8,128)(2,1)}, bf16[32,32,128]{2,1,0:T(8,128)(2,1)}, u32[]{:S(2)}, u32[]{:S(2)}) %collective-permute-start.5) | collective-permute-done | bytes 262176 | tf_op jit(solution)/shard_map/ppermute | solution.py:96
  92.1 2.2 %fusion.6 = bf16[32,32,128]{2,1,0:T(8,128)(2,1)} fusion(bf16[32,32,128]{2,1,0:T(8,128)(2,1)} %collective-permute-done.6, bf16[32,32,128]{2,1,0:T(8,128)(2,1)} %collective-permute-done.5, bf16[32,32,128]{2,1,0:T(8,128)(2,1)} %collective-permute-done.4, f32[32,4,32,128]{3,2,1,0:T(8,128)} %bitcast.51, s32[]{:T(128)S(6)} %select_n.136), kind=kLoop, calls=%fused_computation.13 | loop fusion | flops 917504 | bytes 1572868 | tf_op jit(solution)/shard_map/convert_element_type | solution.py:101
  94.2 10.7 %all-to-all-start.1 = ((bf16[32,32,128]{2,1,0:T(8,128)(2,1)}), bf16[32,32,128]{2,1,0:T(8,128)(2,1)S(1)}, u32[]{:S(2)}, u32[]{:S(2)}) async-start(bf16[32,32,128]{2,1,0:T(8,128)(2,1)} %fusion.6), calls=%async_computation.1 | async-start | bytes 524288 | tf_op jit(solution)/shard_map/all_to_all | solution.py:100
  104.9 1.1 broadcast_select_fusion.3
  106.1 2.5 %fusion = f32[256,128]{1,0:T(8,128)S(1)} fusion(bf16[256,4096]{0,1:T(8,128)(2,1)} %collective-permute-done.2, bf16[2048,128]{1,0:T(8,128)(2,1)S(1)} %bitcast.56, bf16[2048,128]{1,0:T(8,128)(2,1)S(1)} %bitcast.54), kind=kOutput, calls=%fused_computation.4 | convolution fusion | flops 270532608 | bytes 3276800 | tf_op jit(solution)/shard_map/dot_general | solution.py:108
  108.6 1.9 %collective-permute-start.3 = (f32[256,128]{1,0:T(8,128)S(1)}, f32[256,128]{1,0:T(8,128)S(1)}, u32[]{:S(2)}, u32[]{:S(2)}) collective-permute-start(f32[256,128]{1,0:T(8,128)S(1)} %fusion), channel_id=1, source_target_pairs={{0,1},{1,0},{2,3},{3,2},{4,5},{5,4},{6,7},{7,6},{8,9},{9,8},{10,11... | collective-permute-start | bytes 393224 | tf_op jit(solution)/shard_map/ppermute | solution.py:109
  110.6 4.2 %all-to-all-done.1 = bf16[32,32,128]{2,1,0:T(8,128)(2,1)S(1)} async-done(((bf16[32,32,128]{2,1,0:T(8,128)(2,1)}), bf16[32,32,128]{2,1,0:T(8,128)(2,1)S(1)}, u32[]{:S(2)}, u32[]{:S(2)}) %all-to-all-start.1) | async-done | bytes 262176 | tf_op jit(solution)/shard_map/all_to_all | solution.py:100
  115.6 4.2 %all-to-all-start.2 = ((f32[8,40,128]{2,1,0:T(8,128)}), f32[8,40,128]{2,1,0:T(8,128)S(1)}, u32[]{:S(2)}, u32[]{:S(2)}) async-start(f32[8,40,128]{2,1,0:T(8,128)} %broadcast_in_dim.55), calls=%async_computation.2 | async-start | bytes 327680 | tf_op jit(solution)/shard_map/all_to_all | solution.py:118
  119.8 2.4 %fusion.3 = bf16[256,128]{1,0:T(8,128)(2,1)} fusion(f32[256,128]{1,0:T(8,128)S(1)} %collective-permute-done.3, bf16[256,4096]{0,1:T(8,128)(2,1)S(1)} %bitcast.48, bf16[2048,128]{1,0:T(8,128)(2,1)} %bitcast.57, bf16[2048,128]{1,0:T(8,128)(2,1)S(1)} %bitcast.55), kind=kOutput, calls=%fused_computation.7 | convolution fusion | flops 270598144 | bytes 3342336 | tf_op jit(solution)/shard_map/dot_general | solution.py:107
  122.2 8.2 %all-to-all-done.2 = f32[8,40,128]{2,1,0:T(8,128)S(1)} async-done(((f32[8,40,128]{2,1,0:T(8,128)}), f32[8,40,128]{2,1,0:T(8,128)S(1)}, u32[]{:S(2)}, u32[]{:S(2)}) %all-to-all-start.2) | async-done | bytes 163872 | tf_op jit(solution)/shard_map/all_to_all | solution.py:118
  (48 shorter events, 7.3 us)
Async XLA Ops:
  10.9 14.7 %collective-permute-start = (bf16[272,128]{1,0:T(8,128)(2,1)S(1)}, bf16[272,128]{1,0:T(8,128)(2,1)S(1)}, u32[]{:S(2)}, u32[]{:S(2)}) collective-permute-start(bf16[272,128]{1,0:T(8,128)(2,1)S(1)} %pad_maximum_fusion.7), channel_id=1, source_target_pairs={{0,1},{1,0},{2,3},{3,2},{4,5},{5,4},{6,7},{7,6},{8,9},{9,8},{10,11... | collective-permute-start | bytes 208904 | tf_op jit(solution)/shard_map/ppermute | solution.py:54
  19.3 13.2 %copy-start.4 = (bf16[128,128]{1,0:T(8,128)(2,1)S(1)}, bf16[128,128]{1,0:T(8,128)(2,1)}, u32[]{:S(2)}) copy-start(bf16[128,128]{1,0:T(8,128)(2,1)} %param.7) | copy-start | bytes 98308
  23.1 44.8 %copy-start.3 = (bf16[256,128]{1,0:T(8,128)(2,1)S(1)}, bf16[256,128]{1,0:T(8,128)(2,1)}, u32[]{:S(2)}) copy-start(bf16[256,128]{1,0:T(8,128)(2,1)} %param.8) | copy-start | bytes 196612
  23.1 45.6 %collective-permute-start.2 = (bf16[256,4096]{0,1:T(8,128)(2,1)}, bf16[256,4096]{0,1:T(8,128)(2,1)}, u32[]{:S(2)}, u32[]{:S(2)}) collective-permute-start(bf16[256,4096]{0,1:T(8,128)(2,1)} %bitcast.11), channel_id=1, source_target_pairs={{0,1},{1,0},{2,3},{3,2},{4,5},{5,4},{6,7},{7,6},{8,9},{9,8},{10,11... | collective-permute-start | bytes 6291464 | tf_op jit(solution)/shard_map/ppermute | solution.py:60
  33.4 28.2 %all-to-all-start = ((bf16[16,144,128]{2,1,0:T(8,128)(2,1)}), bf16[16,144,128]{2,1,0:T(8,128)(2,1)S(1)}, u32[]{:S(2)}, u32[]{:S(2)}) async-start(bf16[16,144,128]{2,1,0:T(8,128)(2,1)} %broadcast_in_dim.50), calls=%async_computation | async-start | bytes 1179648 | tf_op jit(solution)/shard_map/all_to_all | solution.py:64
  63.9 21.5 %collective-permute-start.1 = (bf16[16,144,128]{2,1,0:T(8,128)(2,1)S(1)}, bf16[16,144,128]{2,1,0:T(8,128)(2,1)S(1)}, u32[]{:S(2)}, u32[]{:S(2)}) collective-permute-start(bf16[16,144,128]{2,1,0:T(8,128)(2,1)S(1)} %all-to-all-done), channel_id=1, source_target_pairs={{0,304},{16,32},{32,16},{48,256},{256,48},{272,288},{288,272},{304... | collective-permute-start | bytes 1769480 | tf_op jit(solution)/shard_map/ppermute | solution.py:71
  71.1 1.3 copy-start
  73.4 15.6 %collective-permute-start.6 = (bf16[32,32,128]{2,1,0:T(8,128)(2,1)}, bf16[32,32,128]{2,1,0:T(8,128)(2,1)}, u32[]{:S(2)}, u32[]{:S(2)}) collective-permute-start(bf16[32,32,128]{2,1,0:T(8,128)(2,1)} %get-tuple-element.9), channel_id=1, source_target_pairs={{0,192},{64,0},{128,64},{192,128},{1,193},{65,1},{129,65},{193,129... | collective-permute-start | bytes 786440 | tf_op jit(solution)/shard_map/ppermute | solution.py:96
  78.0 14.0 %collective-permute-start.5 = (bf16[32,32,128]{2,1,0:T(8,128)(2,1)}, bf16[32,32,128]{2,1,0:T(8,128)(2,1)}, u32[]{:S(2)}, u32[]{:S(2)}) collective-permute-start(bf16[32,32,128]{2,1,0:T(8,128)(2,1)} %get-tuple-element.10), channel_id=1, source_target_pairs={{0,64},{64,128},{128,192},{192,0},{1,65},{65,129},{129,193},{193,1... | collective-permute-start | bytes 786440 | tf_op jit(solution)/shard_map/ppermute | solution.py:96
  80.0 12.1 %collective-permute-start.4 = (bf16[32,32,128]{2,1,0:T(8,128)(2,1)S(1)}, bf16[32,32,128]{2,1,0:T(8,128)(2,1)}, u32[]{:S(2)}, u32[]{:S(2)}) collective-permute-start(bf16[32,32,128]{2,1,0:T(8,128)(2,1)S(1)} %get-tuple-element.8), channel_id=1, source_target_pairs={{0,128},{64,192},{128,0},{192,64},{1,129},{65,193},{129,1},{193,65... | collective-permute-start | bytes 786440 | tf_op jit(solution)/shard_map/ppermute | solution.py:96
  85.4 8.8 %copy-start.2 = (bf16[16,144,128]{2,1,0:T(8,128)(2,1)}, bf16[16,144,128]{2,1,0:T(8,128)(2,1)S(1)}, u32[]{:S(2)}) copy-start(bf16[16,144,128]{2,1,0:T(8,128)(2,1)S(1)} %collective-permute-done.1) | copy-start | bytes 1769476
  94.2 20.5 %all-to-all-start.1 = ((bf16[32,32,128]{2,1,0:T(8,128)(2,1)}), bf16[32,32,128]{2,1,0:T(8,128)(2,1)S(1)}, u32[]{:S(2)}, u32[]{:S(2)}) async-start(bf16[32,32,128]{2,1,0:T(8,128)(2,1)} %fusion.6), calls=%async_computation.1 | async-start | bytes 524288 | tf_op jit(solution)/shard_map/all_to_all | solution.py:100
  106.0 2.6 %copy-start.1 = (bf16[16,128,128]{2,1,0:T(8,128)(2,1)}, bf16[16,128,128]{2,1,0:T(8,128)(2,1)S(1)}, u32[]{:S(2)}) copy-start(bf16[16,128,128]{2,1,0:T(8,128)(2,1)S(1)} %get-tuple-element.12) | copy-start | bytes 1572868
  106.1 8.8 %copy-start.5 = (f32[40]{0:T(128)S(1)}, f32[40]{0:T(128)}, u32[]{:S(2)}) copy-start(f32[40]{0:T(128)} %pad.7.clone) | copy-start | bytes 484
  106.1 8.8 %copy-start.6 = (f32[40]{0:T(128)S(1)}, f32[40]{0:T(128)}, u32[]{:S(2)}) copy-start(f32[40]{0:T(128)} %pad.5.clone) | copy-start | bytes 484
  108.6 11.2 %collective-permute-start.3 = (f32[256,128]{1,0:T(8,128)S(1)}, f32[256,128]{1,0:T(8,128)S(1)}, u32[]{:S(2)}, u32[]{:S(2)}) collective-permute-start(f32[256,128]{1,0:T(8,128)S(1)} %fusion), channel_id=1, source_target_pairs={{0,1},{1,0},{2,3},{3,2},{4,5},{5,4},{6,7},{7,6},{8,9},{9,8},{10,11... | collective-permute-start | bytes 393224 | tf_op jit(solution)/shard_map/ppermute | solution.py:109
  115.6 14.9 %all-to-all-start.2 = ((f32[8,40,128]{2,1,0:T(8,128)}), f32[8,40,128]{2,1,0:T(8,128)S(1)}, u32[]{:S(2)}, u32[]{:S(2)}) async-start(f32[8,40,128]{2,1,0:T(8,128)} %broadcast_in_dim.55), calls=%async_computation.2 | async-start | bytes 327680 | tf_op jit(solution)/shard_map/all_to_all | solution.py:118

commit v2 on v0

v2 whole, which is shorter than its diff:
```python
import functools

import jax
import jax.numpy as jnp
from jax import lax
from jax.experimental import pallas as pl
from jax.experimental.pallas import tpu as pltpu
from jax.sharding import Mesh, PartitionSpec as P

SEQ = 4096
BETA = 0.1
HEAD = 128
EXTRA = 16
PAIRS = 16
ROWS = 256
WIDTH = 8192
HALF = WIDTH // 2
BLOCKS = HALF // HEAD
XS, ZS = 4, 8
SHARE = HEAD // XS
NEAR = 2 * ZS

SIZES = (("yh", 2), ("x", XS), ("yp", 2), ("yq", 2), ("z", ZS), ("c", 2))
NAMES = tuple(name for name, _ in SIZES)
DP = ("yh", "x")
FSDP = ("yp", "yq", "z", "c")
SWAP = ((0, 1), (1, 0))
F32, BF16 = jnp.float32, jnp.bfloat16

VMEM = pl.BlockSpec(memory_space=pltpu.VMEM)
SMEM = pl.BlockSpec(memory_space=pltpu.SMEM)


def local(kernel, out_shape, in_specs, *args, flops=0, moved=0, megabytes=8, **more):
    return pl.pallas_call(
        kernel,
        out_shape=out_shape,
        in_specs=in_specs,
        compiler_params=pltpu.CompilerParams(vmem_limit_bytes=megabytes << 20),
        cost_estimate=pl.CostEstimate(flops=flops, bytes_accessed=moved, transcendentals=0),
        **more,
    )(*args)


def shape(dims, kind):
    return jax.ShapeDtypeStruct(dims, kind)


def prompt_of(prompt_ref):
    pair = (lax.axis_index("yh") * XS + lax.axis_index("x")) * 2 + lax.axis_index("yp")
    return prompt_ref[pair]


def offset_of(core):
    return (lax.axis_index("z") * 2 + core) * ROWS


def total_kernel(prompt_ref, policy_ref, reference_ref, out_ref):
    at = lax.broadcasted_iota(jnp.int32, (2, HEAD), 0) * HEAD + lax.broadcasted_iota(jnp.int32, (2, HEAD), 1)
    mask = offset_of(lax.axis_index("c")) + at >= prompt_of(prompt_ref)
    part = jnp.sum(jnp.where(mask, policy_ref[...] - reference_ref[...], 0.0))
    out_ref[...] = jnp.full((8, HEAD), part, F32)


def pack_kernel(weight_ref, own_ref, other_ref, out_ref):
    part = own_ref[0:1] + other_ref[0:1]
    high = part.astype(BF16).astype(F32)
    middle = (part - high).astype(BF16).astype(F32)
    low = (part - high) - middle
    row = lax.broadcasted_iota(jnp.int32, (EXTRA, HEAD), 0)
    tile = jnp.where(row == 0, high, jnp.where(row == 1, middle, jnp.where(row == 2, low, 0.0))).astype(BF16)
    for chip in range(NEAR):
        out_ref[chip, :HEAD] = weight_ref[...]
        out_ref[chip, HEAD:] = tile


def split_kernel(act_ref, sens_ref, own_ref, send_ref):
    def move(parity):
        for block in range(BLOCKS):
            to = slice(block * HEAD, (block + 1) * HEAD)
            mine, theirs = (2 * block + parity) * HEAD, (2 * block + 1 - parity) * HEAD
            own_ref[:, to] = act_ref[:, mine : mine + HEAD]
            send_ref[:, to] = act_ref[:, theirs : theirs + HEAD]

    core = lax.axis_index("c")
    pl.when(core == 0)(lambda: move(0))
    pl.when(core == 1)(lambda: move(1))
    send_ref[:, HALF:] = sens_ref[...]


def margin_of(tiles):
    terms = tiles[:, 0:3].astype(F32)
    by_chip = jnp.sum(terms, axis=1)
    chosen = jnp.sum(by_chip[:ZS], axis=0, keepdims=True)
    rejected = jnp.sum(by_chip[ZS:], axis=0, keepdims=True)
    return BETA * (chosen - rejected)


def grad_kernel(prompt_ref, near_ref, own_ref, other_ref, sens_ref, keep_ref, one_ref, two_ref, three_ref, grad_ref):
    margin = margin_of(near_ref[...])
    pair_scale = -BETA * (1.0 / (1.0 + jnp.exp(margin))) / PAIRS
    scale = jnp.where(lax.axis_index("yq") == 0, pair_scale, -pair_scale)
    prompt = prompt_of(prompt_ref)
    core = lax.axis_index("c")
    token = lax.broadcasted_iota(jnp.int32, (ROWS, HEAD), 0)

    def cotangent(sens, index):
        token_scale = jnp.where(offset_of(index) + token >= prompt, scale, 0.0)
        return (token_scale * sens.astype(F32)).astype(BF16).astype(F32).T.astype(BF16)

    mine = cotangent(sens_ref[...], core)
    theirs = cotangent(other_ref[:, HALF:], 1 - core)
    x = lax.axis_index("x")
    step = 512
    for start in range(0, HALF, step):
        to = slice(start, start + step)
        grad_ref[...] = jnp.dot(mine, own_ref[:, to], preferred_element_type=F32) + jnp.dot(
            theirs, other_ref[:, to], preferred_element_type=F32
        )
        def rows(distance):
            return grad_ref[pl.ds(pl.multiple_of(lax.rem(x + distance, XS) * SHARE, SHARE), SHARE), :]
        keep_ref[:, to] = rows(0)
        for distance, ref in ((1, one_ref), (2, two_ref), (3, three_ref)):
            ref[:, to] = rows(distance).astype(BF16)


def add_kernel(keep_ref, one_ref, two_ref, three_ref, out_ref):
    for block in range(BLOCKS):
        at = slice(block * HEAD, (block + 1) * HEAD)
        total = keep_ref[:, at]
        for ref in (one_ref, two_ref, three_ref):
            total = total + ref[:, at].astype(F32)
        out_ref[block] = total.astype(BF16)


def project_kernel(near_ref, far_ref, own_ref, other_ref, mine_ref, theirs_ref):
    yp = lax.axis_index("yp")
    mine = jnp.zeros((ROWS, HEAD), F32)
    theirs = jnp.zeros((ROWS, HEAD), F32)
    for ref, index in ((near_ref, yp), (far_ref, 1 - yp)):
        for chip in range(0, NEAR, 2):
            weight = jnp.concatenate([ref[chip, :HEAD], ref[chip + 1, :HEAD]])
            at = pl.ds(pl.multiple_of(index * (HALF // 2) + chip * HEAD, HEAD), 2 * HEAD)
            mine += jnp.dot(own_ref[:, at], weight, preferred_element_type=F32)
            theirs += jnp.dot(other_ref[:, at], weight, preferred_element_type=F32)
    mine_ref[...] = mine
    theirs_ref[...] = theirs


def join_kernel(terms_ref, near_ref, far_ref, out_ref):
    total = jnp.sum(terms_ref[...].astype(F32), axis=0)
    row = lax.broadcasted_iota(jnp.int32, (8, HEAD), 0)
    tail = jnp.where(row == 0, margin_of(near_ref[...]), margin_of(far_ref[...]))
    for replica in range(2 * XS):
        out_ref[replica, :SHARE] = total
        out_ref[replica, SHARE:] = tail


def last_kernel(shares_ref, grad_ref, margins_ref, loss_ref):
    parts = [shares_ref[x, :SHARE] + shares_ref[XS + x, :SHARE] for x in range(XS)]
    grad_ref[...] = jnp.concatenate(parts).T
    yp, yq = lax.axis_index("yp"), lax.axis_index("yq")
    lane = lax.broadcasted_iota(jnp.int32, (1, HEAD), 1)
    margins = jnp.zeros((1, HEAD), F32)
    for yh in range(2):
        for x in range(XS):
            near = shares_ref[yh * XS + x, SHARE : SHARE + 1]
            flipped = shares_ref[(1 - yh) * XS + x, SHARE + 1 : SHARE + 2]
            straight = shares_ref[yh * XS + x, SHARE + 1 : SHARE + 2]
            far = jnp.where(yp == yq, flipped, straight)
            pair = (yh * XS + x) * 2
            margins = jnp.where(lane == pair + yp, near, margins)
            margins = jnp.where(lane == pair + 1 - yp, far, margins)
    margins_ref[...] = margins[:, :PAIRS]
    losses = jnp.maximum(-margins, 0.0) + jnp.log1p(jnp.exp(-jnp.abs(margins)))
    loss_ref[0, 0] = jnp.sum(jnp.where(lane < PAIRS, losses, 0.0)) / PAIRS


def body(activations, value_weight, sensitivity, policy_logp, reference_logp, prompt_len):
    part = local(
        total_kernel,
        shape((8, HEAD), F32),
        [SMEM, VMEM, VMEM],
        prompt_len, policy_logp.reshape(2, HEAD), reference_logp.reshape(2, HEAD),
        moved=4096,
    )
    part_other = lax.ppermute(part, "c", SWAP)
    height = HEAD + EXTRA
    packed = local(
        pack_kernel,
        shape((NEAR, height, HEAD), BF16),
        [VMEM] * 3,
        value_weight, part, part_other,
        moved=600 << 10,
    )
    near = lax.all_to_all(packed.reshape(-1, HEAD), ("yq", "z"), 0, 0, tiled=True).reshape(NEAR, height, HEAD)
    outside = [(y, (y + 1) % 8 if y % 2 else (y - 1) % 8) for y in range(8)]
    far = lax.ppermute(near, ("yh", "yp", "yq"), outside)

    strip = ROWS // 4
    own, send = local(
        split_kernel,
        (shape((ROWS, HALF), BF16), shape((ROWS, HALF + HEAD), BF16)),
        [pl.BlockSpec((strip, WIDTH), lambda i: (i, 0)), pl.BlockSpec((strip, HEAD), lambda i: (i, 0))],
        activations, sensitivity,
        moved=8 << 20,
        grid=(4,),
        out_specs=(
            pl.BlockSpec((strip, HALF), lambda i: (i, 0)),
            pl.BlockSpec((strip, HALF + HEAD), lambda i: (i, 0)),
        ),
    )
    other = lax.ppermute(send, "c", SWAP)

    tile = pl.BlockSpec((NEAR, EXTRA, HEAD), lambda i: (0, HEAD // EXTRA, 0))
    whole = lambda dims: pl.BlockSpec(dims, lambda i: (0,) * len(dims))
    keep, one, two, three = local(
        grad_kernel,
        (shape((SHARE, HALF), F32),) + (shape((SHARE, HALF), BF16),) * 3,
        [SMEM, tile, whole((ROWS, HALF)), whole((ROWS, HALF + HEAD)), whole((ROWS, HEAD))],
        prompt_len, near, own, other, sensitivity,
        flops=2 * 2 * ROWS * HALF * HEAD, moved=6 << 20, megabytes=24,
        grid=(1,),
        out_specs=(whole((SHARE, HALF)),) * 4,
        scratch_shapes=[pltpu.VMEM((HEAD, 512), F32)],
    )
    sent = [
        lax.ppermute(chunk, "x", [(i, (i + step) % XS) for i in range(XS)])
        for step, chunk in ((1, one), (2, two), (3, three))
    ]
    summed = local(add_kernel, shape((BLOCKS, SHARE, HEAD), BF16), [VMEM] * 4, keep, *sent, moved=2 << 20)
    terms = lax.all_to_all(summed.reshape(-1, HEAD), ("yp", "yq", "z"), 0, 0, tiled=True)

    mine, theirs = local(
        project_kernel,
        (shape((ROWS, HEAD), F32),) * 2,
        [VMEM] * 4,
        near, far, own, other,
        flops=2 * 2 * ROWS * HALF * HEAD, moved=6 << 20, megabytes=24,
    )
    projected = (mine + lax.ppermute(theirs, "c", SWAP)).astype(BF16)

    high = SHARE + 8
    joined = local(
        join_kernel,
        shape((2 * XS, high, HEAD), F32),
        [whole((BLOCKS, SHARE, HEAD)), tile, tile],
        terms.reshape(BLOCKS, SHARE, HEAD), near, far,
        moved=1 << 20,
        grid=(1,),
        out_specs=whole((2 * XS, high, HEAD)),
    )
    shares = lax.all_to_all(joined.reshape(-1, HEAD), DP, 0, 0, tiled=True).reshape(2 * XS, high, HEAD)
    weight_grad, margins, loss = local(
        last_kernel,
        (shape((HEAD, HEAD), F32), shape((1, PAIRS), F32), shape((1, 1), F32)),
        [VMEM],
        shares,
        moved=300 << 10,
        out_specs=(VMEM, VMEM, SMEM),
    )
    return projected, weight_grad, margins.reshape(PAIRS), loss.reshape(())


def solution(mesh):
    devices = mesh.devices.reshape(tuple(size for _, size in SIZES))
    return jax.shard_map(
        body,
        mesh=Mesh(devices, NAMES),
        in_specs=(
            P(DP + FSDP, None),
            P(FSDP, None),
            P(DP + FSDP, None),
            P(DP + FSDP),
            P(DP + FSDP),
            P(),
        ),
        out_specs=(P(DP + FSDP, None), P(FSDP, None), P(), P()),
        check_vma=False,
    )
```

time: 701 us -> 101 us (0.14)
  waiting for transfers between devices: 526 us -> 20.1 us
  blocking collectives: 145 us -> 30.3 us
  starting transfers between devices: 0.12 us -> 34.9 us
  between operations: 15.5 us -> 0.82 us
  matrix products: 9.73 us -> 0 us
  Pallas kernels: 0 us -> 7.75 us
    reduce_scatter x1 -> x0, waiting for transfers between devices: 265 us -> none  [body(): lax.psum_scatter(lax.dot_general(columns, cotangent, (((0,), (0,)), ((),...]
    all_gather x1 -> x0, waiting for transfers between devices: 153 us -> none  [body(): lax.all_gather(value_weight, 'fsdp', axis=0, tiled=True)]
    psum x2 -> x0, blocking collectives: 145 us -> none  [the longest x1 113 us: body(): group_totals = lax.psum(partial_totals, 'fsdp')]
    psum x1 -> x0, waiting for transfers between devices: 107 us -> none  [body(): weight_grad = lax.psum(owned, 'dp')]
    all_to_all x0 -> x1, blocking collectives: none -> 30.3 us  [body(): lax.all_to_all(packed.reshape(-1, HEAD), ('yq', 'z'), 0, 0, tiled=True)]
    ppermute x0 -> x7, starting transfers between devices: none -> 21 us  [the longest x3 11.4 us: body(): lax.ppermute(chunk, 'x', [(i, (i + step) % XS) for i in range(XS)])]
    all_to_all x0 -> x2, starting transfers between devices: none -> 14 us  [the longest x1 7.84 us: body(): lax.all_to_all(joined.reshape(-1, HEAD), DP, 0, 0, tiled=True)]
    all_to_all x0 -> x2, waiting for transfers between devices: none -> 11.6 us  [the longest x1 10.3 us: body(): lax.all_to_all(joined.reshape(-1, HEAD), DP, 0, 0, tiled=True)]
  transfers between devices with their start and end apart: 3 -> 9, of which waited for: 3 -> 6; matrix products, arithmetic and copies ran while one was open for 1% -> 1% of each run, Pallas kernels for 0% -> 4%
where the time goes in v2:
time: 101 us; the launch traced here: 99.9 us
  starting transfers between devices  34.9 us (35%)
  blocking collectives  30.3 us (30%)
  waiting for transfers between devices  20.1 us (20%)
  Pallas kernels  7.75 us (8%)
  local copies, waits for them, and re-layouts  5.33 us (5%)
    all_to_all x1, blocking collectives, body(): lax.all_to_all(packed.reshape(-1, HEAD), ('yq', 'z'), 0, 0, tiled=True)  30.3 us
    ppermute x3, starting transfers between devices, body(): lax.ppermute(chunk, 'x', [(i, (i + step) % XS) for i in range(XS)])  11.4 us
    all_to_all x1, waiting for transfers between devices, body(): lax.all_to_all(joined.reshape(-1, HEAD), DP, 0, 0, tiled=True)  10.3 us
    all_to_all x1, starting transfers between devices, body(): lax.all_to_all(joined.reshape(-1, HEAD), DP, 0, 0, tiled=True)  7.84 us
    pallas_call x8, Pallas kernels, local(): pl.pallas_call(kernel, out_shape=out_shape, in_specs=in_specs, compiler_p...  7.75 us
    all_to_all x1, starting transfers between devices, body(): lax.all_to_all(summed.reshape(-1, HEAD), ('yp', 'yq', 'z'), 0, 0, tiled=T...  6.14 us
    unnamed x20, local copies, waits for them, and re-layouts  5.33 us
    ppermute x3, waiting for transfers between devices, body(): lax.ppermute(chunk, 'x', [(i, (i + step) % XS) for i in range(XS)])  4.08 us
  transfers between devices with their start and end apart: 9, of which 6 were waited for; matrix products, arithmetic and copies ran while one was open for 1% of the time, Pallas kernels for 4%

profile of v2, /device:TPU:8, one launch (start us, length us, event | category | flops | bytes accessed | tf_op | source)
XLA Modules:
  0.0 99.9 jit_solution(12719554599238399881)
XLA Ops:
  0.6 2.2 %copy-done.2 = bf16[256,8192]{1,0:T(8,128)(2,1)S(1)} copy-done((bf16[256,8192]{1,0:T(8,128)(2,1)S(1)}, bf16[256,8192]{1,0:T(8,128)(2,1)}, u32[]{:S(2)}) %copy-start.2) | copy-done | bytes 4194328
  2.8 0.8 copy-done.4
  3.7 0.9 shard_map.95
  4.6 1.9 %collective-permute-start.2 = (bf16[256,4224]{1,0:T(8,128)(2,1)S(1)}, bf16[256,4224]{1,0:T(8,128)(2,1)S(1)}, u32[]{:S(2)}, u32[]{:S(2)}) collective-permute-start(bf16[256,4224]{1,0:T(8,128)(2,1)S(1)} %get-tuple-element.16), channel_id=1, source_target_pairs={{0,1},{1,0},{2,3},{3,2},{4,5},{5,4},{6,7},{7,6},{8,9},{9,8},{10,11... | collective-permute-start | bytes 6488072 | tf_op jit(solution)/shard_map/ppermute | solution.py:213
  6.5 0.7 shard_map.93.own_ref
  7.2 2.4 %collective-permute-start = (f32[8,128]{1,0:T(8,128)S(1)}, f32[8,128]{1,0:T(8,128)S(1)}, u32[]{:S(2)}, u32[]{:S(2)}) collective-permute-start(f32[8,128]{1,0:T(8,128)S(1)} %shard_map.93.own_ref), channel_id=1, source_target_pairs={{0,1},{1,0},{2,3},{3,2},{4,5},{5,4},{6,7},{7,6},{8,9},{9,8},{10,11... | collective-permute-start | bytes 12296 | tf_op jit(solution)/shard_map/ppermute | solution.py:187
  9.6 1.1 %collective-permute-done.other_ref = f32[8,128]{1,0:T(8,128)S(1)} collective-permute-done((f32[8,128]{1,0:T(8,128)S(1)}, f32[8,128]{1,0:T(8,128)S(1)}, u32[]{:S(2)}, u32[]{:S(2)}) %collective-permute-start) | collective-permute-done | bytes 4128 | tf_op jit(solution)/shard_map/ppermute | solution.py:187
  10.7 0.1 shard_map.94
  10.8 30.3 %all_to_all.18.near_ref = bf16[16,144,128]{2,1,0:T(8,128)(2,1)S(1)} all-to-all(bf16[16,144,128]{2,1,0:T(8,128)(2,1)S(1)} %shard_map.94), channel_id=1, replica_groups=mesh['yh'=2,'x'=4,'yp'=2,'yq'=2,'z'=8,'c'=2] {'yq','z'}, dimensions={0} | all-to-all | bytes 1179648 | tf_op jit(solution)/shard_map/all_to_all | solution.py:196
  41.1 0.0 collective-permute-done.2.other_ref
  41.2 1.6 %shard_map.97 = (f32[32,4096]{1,0:T(8,128)S(1)}, bf16[32,4096]{1,0:T(8,128)(2,1)S(1)}, bf16[32,4096]{1,0:T(8,128)(2,1)S(1)}, bf16[32,4096]{1,0:T(8,128)(2,1)S(1)}) custom-call(s32[16]{0:T(128)S(1)} %copy-done.7, bf16[16,144,128]{2,1,0:T(8,128)(2,1)S(1)} %all_to_all.18.near_ref, bf16[256,4096]{1,0:T(8,128)(2,1)S(1)} %get-tuple-element.15.own_ref, ...), custom_call_target="tpu_custom_call" | custom-call | flops 536870912 | bytes 6291456 | tf_op jit(solution)/shard_map/pallas_call | solution.py:35
  42.7 3.4 %collective-permute-start.4 = (bf16[32,4096]{1,0:T(8,128)(2,1)S(1)}, bf16[32,4096]{1,0:T(8,128)(2,1)S(1)}, u32[]{:S(2)}, u32[]{:S(2)}) collective-permute-start(bf16[32,4096]{1,0:T(8,128)(2,1)S(1)} %get-tuple-element.20), channel_id=1, source_target_pairs={{0,64},{64,128},{128,192},{192,0},{1,65},{65,129},{129,193},{193,1... | collective-permute-start | bytes 786440 | tf_op jit(solution)/shard_map/ppermute | solution.py:228
  46.1 4.6 %collective-permute-start.5 = (bf16[32,4096]{1,0:T(8,128)(2,1)S(1)}, bf16[32,4096]{1,0:T(8,128)(2,1)S(1)}, u32[]{:S(2)}, u32[]{:S(2)}) collective-permute-start(bf16[32,4096]{1,0:T(8,128)(2,1)S(1)} %get-tuple-element.21), channel_id=1, source_target_pairs={{0,128},{64,192},{128,0},{192,64},{1,129},{65,193},{129,1},{193,65... | collective-permute-start | bytes 786440 | tf_op jit(solution)/shard_map/ppermute | solution.py:228
  50.8 3.3 %collective-permute-start.6 = (bf16[32,4096]{1,0:T(8,128)(2,1)S(1)}, bf16[32,4096]{1,0:T(8,128)(2,1)S(1)}, u32[]{:S(2)}, u32[]{:S(2)}) collective-permute-start(bf16[32,4096]{1,0:T(8,128)(2,1)S(1)} %get-tuple-element.22), channel_id=1, source_target_pairs={{0,192},{64,0},{128,64},{192,128},{1,193},{65,1},{129,65},{193,129... | collective-permute-start | bytes 786440 | tf_op jit(solution)/shard_map/ppermute | solution.py:228
  54.1 3.4 %collective-permute-start.1 = (bf16[16,144,128]{2,1,0:T(8,128)(2,1)S(1)}, bf16[16,144,128]{2,1,0:T(8,128)(2,1)S(1)}, u32[]{:S(2)}, u32[]{:S(2)}) collective-permute-start(bf16[16,144,128]{2,1,0:T(8,128)(2,1)S(1)} %all_to_all.18.near_ref), channel_id=1, source_target_pairs={{0,304},{16,32},{32,16},{48,256},{256,48},{272,288},{288,272},{304... | collective-permute-start | bytes 1769480 | tf_op jit(solution)/shard_map/ppermute | solution.py:198
  57.5 0.0 collective-permute-done.4.one_ref
  57.5 2.6 %collective-permute-done.5.two_ref = bf16[32,4096]{1,0:T(8,128)(2,1)S(1)} collective-permute-done((bf16[32,4096]{1,0:T(8,128)(2,1)S(1)}, bf16[32,4096]{1,0:T(8,128)(2,1)S(1)}, u32[]{:S(2)}, u32[]{:S(2)}) %collective-permute-start.5) | collective-permute-done | bytes 262176 | tf_op jit(solution)/shard_map/ppermute | solution.py:228
  60.1 1.5 %collective-permute-done.6.three_ref = bf16[32,4096]{1,0:T(8,128)(2,1)S(1)} collective-permute-done((bf16[32,4096]{1,0:T(8,128)(2,1)S(1)}, bf16[32,4096]{1,0:T(8,128)(2,1)S(1)}, u32[]{:S(2)}, u32[]{:S(2)}) %collective-permute-start.6) | collective-permute-done | bytes 262176 | tf_op jit(solution)/shard_map/ppermute | solution.py:228
  61.6 0.1 shard_map.98
  61.7 0.7 copy-done.3
  62.4 6.1 %all-to-all-start.1 = ((bf16[32,32,128]{2,1,0:T(8,128)(2,1)}), bf16[32,32,128]{2,1,0:T(8,128)(2,1)}, u32[]{:S(2)}, u32[]{:S(2)}) async-start(bf16[32,32,128]{2,1,0:T(8,128)(2,1)} %copy-done.3), calls=%async_computation.1 | async-start | bytes 524288 | tf_op jit(solution)/shard_map/all_to_all | solution.py:232
  68.6 3.3 %collective-permute-done.1.far_ref = bf16[16,144,128]{2,1,0:T(8,128)(2,1)S(1)} collective-permute-done((bf16[16,144,128]{2,1,0:T(8,128)(2,1)S(1)}, bf16[16,144,128]{2,1,0:T(8,128)(2,1)S(1)}, u32[]{:S(2)}, u32[]{:S(2)}) %collective-permute-start.1) | collective-permute-done | bytes 589856 | tf_op jit(solution)/shard_map/ppermute | solution.py:198
  71.9 1.6 %copy-done.1 = bf16[256,4096]{1,0:T(8,128)(2,1)S(1)} copy-done((bf16[256,4096]{1,0:T(8,128)(2,1)S(1)}, bf16[256,4096]{1,0:T(8,128)(2,1)}, u32[]{:S(2)}) %copy-start.1) | copy-done | bytes 2097176
  73.5 1.9 %shard_map.96 = (f32[256,128]{1,0:T(8,128)S(1)}, f32[256,128]{1,0:T(8,128)}) custom-call(bf16[16,144,128]{2,1,0:T(8,128)(2,1)S(1)} %all_to_all.18.near_ref, bf16[16,144,128]{2,1,0:T(8,128)(2,1)S(1)} %collective-permute-done.1.far_ref, bf16[256,4096]{1,0:T(8,128)(2,1)S(1)} %copy-done.1, bf16[256,4224]{1,0:T(8,128)(2,1)S(1)} %collective-permute-done.2.other_ref), custom_call_target="tpu_custom_call" | custom-call | flops 536870912 | bytes 6291456 | tf_op jit(solution)/shard_map/pallas_call | solution.py:35
  75.4 1.9 %collective-permute-start.3 = (f32[256,128]{1,0:T(8,128)}, f32[256,128]{1,0:T(8,128)S(1)}, u32[]{:S(2)}, u32[]{:S(2)}) collective-permute-start(f32[256,128]{1,0:T(8,128)} %get-tuple-element.18), channel_id=1, source_target_pairs={{0,1},{1,0},{2,3},{3,2},{4,5},{5,4},{6,7},{7,6},{8,9},{9,8},{10,11... | collective-permute-start | bytes 393224 | tf_op jit(solution)/shard_map/ppermute | solution.py:241
  77.3 1.2 %all-to-all-done.1.terms_ref = bf16[32,32,128]{2,1,0:T(8,128)(2,1)} async-done(((bf16[32,32,128]{2,1,0:T(8,128)(2,1)}), bf16[32,32,128]{2,1,0:T(8,128)(2,1)}, u32[]{:S(2)}, u32[]{:S(2)}) %all-to-all-start.1) | async-done | bytes 262176 | tf_op jit(solution)/shard_map/all_to_all | solution.py:232
  78.5 1.7 %shard_map.99 = f32[8,40,128]{2,1,0:T(8,128)} custom-call(bf16[32,32,128]{2,1,0:T(8,128)(2,1)} %all-to-all-done.1.terms_ref, bf16[16,144,128]{2,1,0:T(8,128)(2,1)S(1)} %all_to_all.18.near_ref, bf16[16,144,128]{2,1,0:T(8,128)(2,1)S(1)} %collective-permute-done.1.far_ref), custom_call_target="tpu_custom_call" | custom-call | bytes 1048576 | tf_op jit(solution)/shard_map/pallas_call | solution.py:35
  80.2 7.8 %all-to-all-start.2 = ((f32[8,40,128]{2,1,0:T(8,128)}), f32[8,40,128]{2,1,0:T(8,128)S(1)}, u32[]{:S(2)}, u32[]{:S(2)}) async-start(f32[8,40,128]{2,1,0:T(8,128)} %shard_map.99), calls=%async_computation.2 | async-start | bytes 327680 | tf_op jit(solution)/shard_map/all_to_all | solution.py:253
  88.1 0.0 collective-permute-done.3
  88.1 0.6 add_convert_fusion
  88.7 10.3 %all-to-all-done.2.shares_ref = f32[8,40,128]{2,1,0:T(8,128)S(1)} async-done(((f32[8,40,128]{2,1,0:T(8,128)}), f32[8,40,128]{2,1,0:T(8,128)S(1)}, u32[]{:S(2)}, u32[]{:S(2)}) %all-to-all-start.2) | async-done | bytes 163872 | tf_op jit(solution)/shard_map/all_to_all | solution.py:253
  99.1 0.8 shard_map.100
  (16 shorter events, 0.0 us)
Async XLA Ops:
  0.6 2.2 %copy-start.2 = (bf16[256,8192]{1,0:T(8,128)(2,1)S(1)}, bf16[256,8192]{1,0:T(8,128)(2,1)}, u32[]{:S(2)}) copy-start(bf16[256,8192]{1,0:T(8,128)(2,1)} %act_ref.1) | copy-start | bytes 12582916
  2.8 0.8 copy-start.4
  3.7 2.9 %copy-start.7 = (s32[16]{0:T(128)S(1)}, s32[16]{0:T(128)}, u32[]{:S(2)}) copy-start(s32[16]{0:T(128)} %prompt_ref.3) | copy-start | bytes 196
  3.7 2.9 %copy-start.8 = (f32[256]{0:T(256)S(1)}, f32[256]{0:T(256)}, u32[]{:S(2)}) copy-start(f32[256]{0:T(256)} %param.9) | copy-start | bytes 3076
  3.7 2.9 %copy-start.9 = (f32[256]{0:T(256)S(1)}, f32[256]{0:T(256)}, u32[]{:S(2)}) copy-start(f32[256]{0:T(256)} %param.10) | copy-start | bytes 3076
  3.7 7.1 %copy-start.6 = (bf16[128,128]{1,0:T(8,128)(2,1)S(1)}, bf16[128,128]{1,0:T(8,128)(2,1)}, u32[]{:S(2)}) copy-start(bf16[128,128]{1,0:T(8,128)(2,1)} %weight_ref.1) | copy-start | bytes 98308
  3.7 37.5 %copy-start.5 = (bf16[256,128]{1,0:T(8,128)(2,1)S(1)}, bf16[256,128]{1,0:T(8,128)(2,1)}, u32[]{:S(2)}) copy-start(bf16[256,128]{1,0:T(8,128)(2,1)} %sens_ref.3) | copy-start | bytes 196612
  4.6 38.2 %copy-start = (bf16[256,4096]{1,0:T(8,128)(2,1)}, bf16[256,4096]{1,0:T(8,128)(2,1)S(1)}, u32[]{:S(2)}) copy-start(bf16[256,4096]{1,0:T(8,128)(2,1)S(1)} %get-tuple-element.15.own_ref) | copy-start | bytes 6291460
  4.6 36.6 %collective-permute-start.2 = (bf16[256,4224]{1,0:T(8,128)(2,1)S(1)}, bf16[256,4224]{1,0:T(8,128)(2,1)S(1)}, u32[]{:S(2)}, u32[]{:S(2)}) collective-permute-start(bf16[256,4224]{1,0:T(8,128)(2,1)S(1)} %get-tuple-element.16), channel_id=1, source_target_pairs={{0,1},{1,0},{2,3},{3,2},{4,5},{5,4},{6,7},{7,6},{8,9},{9,8},{10,11... | collective-permute-start | bytes 6488072 | tf_op jit(solution)/shard_map/ppermute | solution.py:213
  7.2 3.5 %collective-permute-start = (f32[8,128]{1,0:T(8,128)S(1)}, f32[8,128]{1,0:T(8,128)S(1)}, u32[]{:S(2)}, u32[]{:S(2)}) collective-permute-start(f32[8,128]{1,0:T(8,128)S(1)} %shard_map.93.own_ref), channel_id=1, source_target_pairs={{0,1},{1,0},{2,3},{3,2},{4,5},{5,4},{6,7},{7,6},{8,9},{9,8},{10,11... | collective-permute-start | bytes 12296 | tf_op jit(solution)/shard_map/ppermute | solution.py:187
  42.7 14.8 %collective-permute-start.4 = (bf16[32,4096]{1,0:T(8,128)(2,1)S(1)}, bf16[32,4096]{1,0:T(8,128)(2,1)S(1)}, u32[]{:S(2)}, u32[]{:S(2)}) collective-permute-start(bf16[32,4096]{1,0:T(8,128)(2,1)S(1)} %get-tuple-element.20), channel_id=1, source_target_pairs={{0,64},{64,128},{128,192},{192,0},{1,65},{65,129},{129,193},{193,1... | collective-permute-start | bytes 786440 | tf_op jit(solution)/shard_map/ppermute | solution.py:228
  46.1 13.9 %collective-permute-start.5 = (bf16[32,4096]{1,0:T(8,128)(2,1)S(1)}, bf16[32,4096]{1,0:T(8,128)(2,1)S(1)}, u32[]{:S(2)}, u32[]{:S(2)}) collective-permute-start(bf16[32,4096]{1,0:T(8,128)(2,1)S(1)} %get-tuple-element.21), channel_id=1, source_target_pairs={{0,128},{64,192},{128,0},{192,64},{1,129},{65,193},{129,1},{193,65... | collective-permute-start | bytes 786440 | tf_op jit(solution)/shard_map/ppermute | solution.py:228
  50.8 10.8 %collective-permute-start.6 = (bf16[32,4096]{1,0:T(8,128)(2,1)S(1)}, bf16[32,4096]{1,0:T(8,128)(2,1)S(1)}, u32[]{:S(2)}, u32[]{:S(2)}) collective-permute-start(bf16[32,4096]{1,0:T(8,128)(2,1)S(1)} %get-tuple-element.22), channel_id=1, source_target_pairs={{0,192},{64,0},{128,64},{192,128},{1,193},{65,1},{129,65},{193,129... | collective-permute-start | bytes 786440 | tf_op jit(solution)/shard_map/ppermute | solution.py:228
  54.1 17.7 %collective-permute-start.1 = (bf16[16,144,128]{2,1,0:T(8,128)(2,1)S(1)}, bf16[16,144,128]{2,1,0:T(8,128)(2,1)S(1)}, u32[]{:S(2)}, u32[]{:S(2)}) collective-permute-start(bf16[16,144,128]{2,1,0:T(8,128)(2,1)S(1)} %all_to_all.18.near_ref), channel_id=1, source_target_pairs={{0,304},{16,32},{32,16},{48,256},{256,48},{272,288},{288,272},{304... | collective-permute-start | bytes 1769480 | tf_op jit(solution)/shard_map/ppermute | solution.py:198
  61.7 0.7 copy-start.3
  62.4 16.1 %all-to-all-start.1 = ((bf16[32,32,128]{2,1,0:T(8,128)(2,1)}), bf16[32,32,128]{2,1,0:T(8,128)(2,1)}, u32[]{:S(2)}, u32[]{:S(2)}) async-start(bf16[32,32,128]{2,1,0:T(8,128)(2,1)} %copy-done.3), calls=%async_computation.1 | async-start | bytes 524288 | tf_op jit(solution)/shard_map/all_to_all | solution.py:232
  71.9 1.6 %copy-start.1 = (bf16[256,4096]{1,0:T(8,128)(2,1)S(1)}, bf16[256,4096]{1,0:T(8,128)(2,1)}, u32[]{:S(2)}) copy-start(bf16[256,4096]{1,0:T(8,128)(2,1)} %copy-done) | copy-start | bytes 6291460
  75.4 12.7 %collective-permute-start.3 = (f32[256,128]{1,0:T(8,128)}, f32[256,128]{1,0:T(8,128)S(1)}, u32[]{:S(2)}, u32[]{:S(2)}) collective-permute-start(f32[256,128]{1,0:T(8,128)} %get-tuple-element.18), channel_id=1, source_target_pairs={{0,1},{1,0},{2,3},{3,2},{4,5},{5,4},{6,7},{7,6},{8,9},{9,8},{10,11... | collective-permute-start | bytes 393224 | tf_op jit(solution)/shard_map/ppermute | solution.py:241
  80.2 18.8 %all-to-all-start.2 = ((f32[8,40,128]{2,1,0:T(8,128)}), f32[8,40,128]{2,1,0:T(8,128)S(1)}, u32[]{:S(2)}, u32[]{:S(2)}) async-start(f32[8,40,128]{2,1,0:T(8,128)} %shard_map.99), calls=%async_computation.2 | async-start | bytes 327680 | tf_op jit(solution)/shard_map/all_to_all | solution.py:253

commit v3 on v2

--- a/solution.py
+++ b/solution.py
@@ -28,6 +28,7 @@
 F32, BF16 = jnp.float32, jnp.bfloat16
 
 VMEM = pl.BlockSpec(memory_space=pltpu.VMEM)
+ANY = pl.BlockSpec(memory_space=pl.ANY)
 SMEM = pl.BlockSpec(memory_space=pltpu.SMEM)
 
 
@@ -59,57 +60,70 @@
     at = lax.broadcasted_iota(jnp.int32, (2, HEAD), 0) * HEAD + lax.broadcasted_iota(jnp.int32, (2, HEAD), 1)
     mask = offset_of(lax.axis_index("c")) + at >= prompt_of(prompt_ref)
     part = jnp.sum(jnp.where(mask, policy_ref[...] - reference_ref[...], 0.0))
-    out_ref[...] = jnp.full((8, HEAD), part, F32)
-
-
-def pack_kernel(weight_ref, own_ref, other_ref, out_ref):
-    part = own_ref[0:1] + other_ref[0:1]
-    high = part.astype(BF16).astype(F32)
-    middle = (part - high).astype(BF16).astype(F32)
-    low = (part - high) - middle
+    out_ref[...] = jnp.full(out_ref.shape, part, F32)
+
+
+def pack_kernel(weight_ref, parts_ref, one_ref, two_ref, three_ref, out_ref, *same_refs):
+    del one_ref, two_ref, three_ref, same_refs
     row = lax.broadcasted_iota(jnp.int32, (EXTRA, HEAD), 0)
-    tile = jnp.where(row == 0, high, jnp.where(row == 1, middle, jnp.where(row == 2, low, 0.0))).astype(BF16)
+    tile = jnp.zeros((EXTRA, HEAD), F32)
+    for x in range(XS):
+        part = parts_ref[2 * x, 0:1] + parts_ref[2 * x + 1, 0:1]
+        high = part.astype(BF16).astype(F32)
+        middle = (part - high).astype(BF16).astype(F32)
+        for at, value in enumerate((high, middle, (part - high) - middle)):
+            tile = jnp.where(row == 3 * x + at, value, tile)
     for chip in range(NEAR):
         out_ref[chip, :HEAD] = weight_ref[...]
-        out_ref[chip, HEAD:] = tile
-
-
-def split_kernel(act_ref, sens_ref, own_ref, send_ref):
+        out_ref[chip, HEAD:] = tile.astype(BF16)
+
+
+def columns_of(act_ref, out_ref, index):
     def move(parity):
         for block in range(BLOCKS):
-            to = slice(block * HEAD, (block + 1) * HEAD)
-            mine, theirs = (2 * block + parity) * HEAD, (2 * block + 1 - parity) * HEAD
-            own_ref[:, to] = act_ref[:, mine : mine + HEAD]
-            send_ref[:, to] = act_ref[:, theirs : theirs + HEAD]
-
-    core = lax.axis_index("c")
-    pl.when(core == 0)(lambda: move(0))
-    pl.when(core == 1)(lambda: move(1))
-    send_ref[:, HALF:] = sens_ref[...]
-
-
-def margin_of(tiles):
-    terms = tiles[:, 0:3].astype(F32)
-    by_chip = jnp.sum(terms, axis=1)
-    chosen = jnp.sum(by_chip[:ZS], axis=0, keepdims=True)
-    rejected = jnp.sum(by_chip[ZS:], axis=0, keepdims=True)
-    return BETA * (chosen - rejected)
-
-
-def grad_kernel(prompt_ref, near_ref, own_ref, other_ref, sens_ref, keep_ref, one_ref, two_ref, three_ref, grad_ref):
-    margin = margin_of(near_ref[...])
-    pair_scale = -BETA * (1.0 / (1.0 + jnp.exp(margin))) / PAIRS
-    scale = jnp.where(lax.axis_index("yq") == 0, pair_scale, -pair_scale)
+            start = (2 * block + parity) * HEAD
+            out_ref[:, block * HEAD : (block + 1) * HEAD] = act_ref[:, start : start + HEAD]
+
+    pl.when(index == 0)(lambda: move(0))
+    pl.when(index == 1)(lambda: move(1))
+
+
+def send_kernel(act_ref, sens_ref, out_ref):
+    columns_of(act_ref, out_ref, 1 - lax.axis_index("c"))
+    out_ref[:, HALF:] = sens_ref[...]
+
+
+def own_kernel(act_ref, after_ref, out_ref):
+    del after_ref
+    columns_of(act_ref, out_ref, lax.axis_index("c"))
+
+
+def margins_of(tiles):
+    tiles = tiles.astype(F32)
+    chosen, rejected = jnp.sum(tiles[:ZS], axis=0), jnp.sum(tiles[ZS:], axis=0)
+    return [
+        BETA * (jnp.sum(chosen[at : at + 3], axis=0, keepdims=True) - jnp.sum(rejected[at : at + 3], axis=0, keepdims=True))
+        for at in range(0, 3 * XS, 3)
+    ]
+
+
+def pick_x(rows, x):
+    picked = rows[0]
+    for at in range(1, XS):
+        picked = jnp.where(x == at, rows[at], picked)
+    return picked
+
+
+def grad_kernel(prompt_ref, own_ref, other_ref, sens_ref, keep_ref, one_ref, two_ref, three_ref, grad_ref):
     prompt = prompt_of(prompt_ref)
     core = lax.axis_index("c")
     token = lax.broadcasted_iota(jnp.int32, (ROWS, HEAD), 0)
 
-    def cotangent(sens, index):
-        token_scale = jnp.where(offset_of(index) + token >= prompt, scale, 0.0)
-        return (token_scale * sens.astype(F32)).astype(BF16).astype(F32).T.astype(BF16)
-
-    mine = cotangent(sens_ref[...], core)
-    theirs = cotangent(other_ref[:, HALF:], 1 - core)
+    def masked(sens, index):
+        return jnp.where(offset_of(index) + token >= prompt, sens.astype(F32), 0.0).T.astype(BF16)
+
+    mine = masked(sens_ref[...], core)
+    theirs = masked(other_ref[:, HALF:], 1 - core)
     x = lax.axis_index("x")
     step = 512
     for start in range(0, HALF, step):
@@ -124,12 +138,17 @@
             ref[:, to] = rows(distance).astype(BF16)
 
 
-def add_kernel(keep_ref, one_ref, two_ref, three_ref, out_ref):
+def add_kernel(near_ref, keep_ref, one_ref, two_ref, three_ref, out_ref):
+    x = lax.axis_index("x")
+    sign = jnp.where(lax.axis_index("yq") == 0, -BETA / PAIRS, BETA / PAIRS)
+    scales = [sign / (1.0 + jnp.exp(margin)) for margin in margins_of(near_ref[...])]
+    refs = (keep_ref, one_ref, two_ref, three_ref)
+    scale = [pick_x(scales, lax.rem(x + XS - distance, XS)) for distance in range(XS)]
     for block in range(BLOCKS):
         at = slice(block * HEAD, (block + 1) * HEAD)
-        total = keep_ref[:, at]
-        for ref in (one_ref, two_ref, three_ref):
-            total = total + ref[:, at].astype(F32)
+        total = scale[0] * keep_ref[:, at]
+        for distance in range(1, XS):
+            total = total + scale[distance] * refs[distance][:, at].astype(F32)
         out_ref[block] = total.astype(BF16)
 
 
@@ -150,7 +169,8 @@
 def join_kernel(terms_ref, near_ref, far_ref, out_ref):
     total = jnp.sum(terms_ref[...].astype(F32), axis=0)
     row = lax.broadcasted_iota(jnp.int32, (8, HEAD), 0)
-    tail = jnp.where(row == 0, margin_of(near_ref[...]), margin_of(far_ref[...]))
+    x = lax.axis_index("x")
+    tail = jnp.where(row == 0, pick_x(margins_of(near_ref[...]), x), pick_x(margins_of(far_ref[...]), x))
     for replica in range(2 * XS):
         out_ref[replica, :SHARE] = total
         out_ref[replica, SHARE:] = tail
@@ -179,36 +199,31 @@
 def body(activations, value_weight, sensitivity, policy_logp, reference_logp, prompt_len):
     part = local(
         total_kernel,
-        shape((8, HEAD), F32),
+        shape((2 * XS, 8, HEAD), F32),
         [SMEM, VMEM, VMEM],
         prompt_len, policy_logp.reshape(2, HEAD), reference_logp.reshape(2, HEAD),
-        moved=4096,
-    )
-    part_other = lax.ppermute(part, "c", SWAP)
-    height = HEAD + EXTRA
-    packed = local(
-        pack_kernel,
-        shape((NEAR, height, HEAD), BF16),
-        [VMEM] * 3,
-        value_weight, part, part_other,
-        moved=600 << 10,
-    )
-    near = lax.all_to_all(packed.reshape(-1, HEAD), ("yq", "z"), 0, 0, tiled=True).reshape(NEAR, height, HEAD)
-    outside = [(y, (y + 1) % 8 if y % 2 else (y - 1) % 8) for y in range(8)]
-    far = lax.ppermute(near, ("yh", "yp", "yq"), outside)
-
+        moved=40 << 10,
+    )
+    parts = lax.all_to_all(part.reshape(-1, HEAD), ("x", "c"), 0, 0, tiled=True).reshape(2 * XS, 8, HEAD)
     strip = ROWS // 4
-    own, send = local(
-        split_kernel,
-        (shape((ROWS, HALF), BF16), shape((ROWS, HALF + HEAD), BF16)),
-        [pl.BlockSpec((strip, WIDTH), lambda i: (i, 0)), pl.BlockSpec((strip, HEAD), lambda i: (i, 0))],
+    rows_of = lambda width: pl.BlockSpec((strip, width), lambda i: (i, 0))
+    send = local(
+        send_kernel,
+        shape((ROWS, HALF + HEAD), BF16),
+        [rows_of(WIDTH), rows_of(HEAD)],
         activations, sensitivity,
-        moved=8 << 20,
+        moved=6 << 20,
         grid=(4,),
-        out_specs=(
-            pl.BlockSpec((strip, HALF), lambda i: (i, 0)),
-            pl.BlockSpec((strip, HALF + HEAD), lambda i: (i, 0)),
-        ),
+        out_specs=rows_of(HALF + HEAD),
+    )
+    own = local(
+        own_kernel,
+        shape((ROWS, HALF), BF16),
+        [rows_of(WIDTH), ANY],
+        activations, part,
+        moved=6 << 20,
+        grid=(4,),
+        out_specs=rows_of(HALF),
     )
     other = lax.ppermute(send, "c", SWAP)
 
@@ -217,18 +232,40 @@
     keep, one, two, three = local(
         grad_kernel,
         (shape((SHARE, HALF), F32),) + (shape((SHARE, HALF), BF16),) * 3,
-        [SMEM, tile, whole((ROWS, HALF)), whole((ROWS, HALF + HEAD)), whole((ROWS, HEAD))],
-        prompt_len, near, own, other, sensitivity,
+        [SMEM, whole((ROWS, HALF)), whole((ROWS, HALF + HEAD)), whole((ROWS, HEAD))],
+        prompt_len, own, other, sensitivity,
         flops=2 * 2 * ROWS * HALF * HEAD, moved=6 << 20, megabytes=24,
         grid=(1,),
         out_specs=(whole((SHARE, HALF)),) * 4,
         scratch_shapes=[pltpu.VMEM((HEAD, 512), F32)],
     )
+    height = HEAD + EXTRA
+    packed, one, two, three = local(
+        pack_kernel,
+        (shape((NEAR, height, HEAD), BF16),) + (shape((SHARE, HALF), BF16),) * 3,
+        [VMEM] * 2 + [ANY] * 3,
+        value_weight, parts, one, two, three,
+        moved=600 << 10,
+        out_specs=(VMEM, ANY, ANY, ANY),
+        input_output_aliases={2: 1, 3: 2, 4: 3},
+    )
+    near = lax.all_to_all(packed.reshape(-1, HEAD), ("yq", "z"), 0, 0, tiled=True).reshape(NEAR, height, HEAD)
+    outside = [(y, (y + 1) % 8 if y % 2 else (y - 1) % 8) for y in range(8)]
+    far = lax.ppermute(near, ("yh", "yp", "yq"), outside)
+
     sent = [
         lax.ppermute(chunk, "x", [(i, (i + step) % XS) for i in range(XS)])
         for step, chunk in ((1, one), (2, two), (3, three))
     ]
-    summed = local(add_kernel, shape((BLOCKS, SHARE, HEAD), BF16), [VMEM] * 4, keep, *sent, moved=2 << 20)
+    summed = local(
+        add_kernel,
+        shape((BLOCKS, SHARE, HEAD), BF16),
+        [tile, whole((SHARE, HALF))] + [whole((SHARE, HALF))] * 3,
+        near, keep, *sent,
+        moved=2 << 20,
+        grid=(1,),
+        out_specs=whole((BLOCKS, SHARE, HEAD)),
+    )
     terms = lax.all_to_all(summed.reshape(-1, HEAD), ("yp", "yq", "z"), 0, 0, tiled=True)
 
     mine, theirs = local(

time: 101 us -> 99 us (0.980)
  the two profiles are of different devices: /device:TPU:8 before, /device:TPU:72 now
where the time goes in v3:
time: 99 us; the launch traced here: 98.1 us
  starting transfers between devices  51.8 us (52%)
  waiting for transfers between devices  20.7 us (21%)
  Pallas kernels  14.5 us (15%)
  local copies, waits for them, and re-layouts  8.75 us (9%)
  other arithmetic  1.55 us (2%)
    pallas_call x9, Pallas kernels, local(): pl.pallas_call(kernel, out_shape=out_shape, in_specs=in_specs, compiler_p...  14.5 us
    ppermute x3, starting transfers between devices, body(): lax.ppermute(chunk, 'x', [(i, (i + step) % XS) for i in range(XS)])  11.9 us
    all_to_all x1, starting transfers between devices, body(): lax.all_to_all(packed.reshape(-1, HEAD), ('yq', 'z'), 0, 0, tiled=True)  10.9 us
    all_to_all x1, waiting for transfers between devices, body(): lax.all_to_all(joined.reshape(-1, HEAD), DP, 0, 0, tiled=True)  9.23 us
    all_to_all x1, starting transfers between devices, body(): lax.all_to_all(joined.reshape(-1, HEAD), DP, 0, 0, tiled=True)  8.86 us
    unnamed x24, local copies, waits for them, and re-layouts  8.75 us
    all_to_all x1, starting transfers between devices, body(): lax.all_to_all(summed.reshape(-1, HEAD), ('yp', 'yq', 'z'), 0, 0, tiled=T...  8.69 us
    all_to_all x1, waiting for transfers between devices, body(): lax.all_to_all(packed.reshape(-1, HEAD), ('yq', 'z'), 0, 0, tiled=True)  6.1 us
  transfers between devices with their start and end apart: 10, of which 3 were waited for; matrix products, arithmetic and copies ran while one was open for 2% of the time, Pallas kernels for 11%

profile of v3, /device:TPU:72, one launch (start us, length us, event | category | flops | bytes accessed | tf_op | source)
XLA Modules:
  0.0 98.1 jit_solution(16213744598051212216)
XLA Ops:
  0.6 0.0 copy-start
  0.6 2.2 %copy-done = bf16[256,8192]{1,0:T(8,128)(2,1)S(1)} copy-done((bf16[256,8192]{1,0:T(8,128)(2,1)S(1)}, bf16[256,8192]{1,0:T(8,128)(2,1)}, u32[]{:S(2)}) %copy-start) | copy-done | bytes 4194328
  2.8 0.8 copy-done.5
  3.7 2.0 %shard_map.95 = bf16[256,4224]{1,0:T(8,128)(2,1)} custom-call(bf16[256,8192]{1,0:T(8,128)(2,1)S(1)} %copy-done, bf16[256,128]{1,0:T(8,128)(2,1)S(1)} %copy-done.5), custom_call_target="tpu_custom_call" | custom-call | bytes 6291456 | tf_op jit(solution)/shard_map/pallas_call | solution.py:36
  5.7 1.9 %collective-permute-start = (bf16[256,4224]{1,0:T(8,128)(2,1)}, bf16[256,4224]{1,0:T(8,128)(2,1)}, u32[]{:S(2)}, u32[]{:S(2)}) collective-permute-start(bf16[256,4224]{1,0:T(8,128)(2,1)} %shard_map.95), channel_id=1, source_target_pairs={{0,1},{1,0},{2,3},{3,2},{4,5},{5,4},{6,7},{7,6},{8,9},{9,8},{10,11... | collective-permute-start | bytes 6488072 | tf_op jit(solution)/shard_map/ppermute | solution.py:228
  7.6 1.3 %shard_map.93.after_ref = f32[8,8,128]{2,1,0:T(8,128)} custom-call(s32[16]{0:T(128)S(1)} %copy-done.9, f32[2,128]{1,0:T(2,128)S(1)} %bitcast.4, f32[2,128]{1,0:T(2,128)S(1)} %bitcast.5), custom_call_target="tpu_custom_call" | custom-call | bytes 40960 | tf_op jit(solution)/shard_map/pallas_call | solution.py:36
  8.9 4.4 %all-to-all-start = ((f32[8,8,128]{2,1,0:T(8,128)}), f32[8,8,128]{2,1,0:T(8,128)S(1)}, u32[]{:S(2)}, u32[]{:S(2)}) async-start(f32[8,8,128]{2,1,0:T(8,128)} %shard_map.93.after_ref), calls=%async_computation | async-start | bytes 65536 | tf_op jit(solution)/shard_map/all_to_all | solution.py:207
  13.3 2.2 %copy-done.1 = bf16[256,8192]{1,0:T(8,128)(2,1)S(1)} copy-done((bf16[256,8192]{1,0:T(8,128)(2,1)S(1)}, bf16[256,8192]{1,0:T(8,128)(2,1)}, u32[]{:S(2)}) %copy-start.1) | copy-done | bytes 4194328
  15.5 0.4 shard_map.94.own_ref
  16.0 0.4 copy-done.6
  16.4 3.5 %shard_map.96 = (f32[32,4096]{1,0:T(8,128)S(1)}, bf16[32,4096]{1,0:T(8,128)(2,1)}, bf16[32,4096]{1,0:T(8,128)(2,1)}, bf16[32,4096]{1,0:T(8,128)(2,1)}) custom-call(s32[16]{0:T(128)S(1)} %copy-done.9, bf16[256,4096]{1,0:T(8,128)(2,1)S(1)} %shard_map.94.own_ref, bf16[256,4224]{1,0:T(8,128)(2,1)} %collective-permute-done.other_ref, bf16[256,128]{1,0:T(8,128)(2,1)S(1)} %copy-done.6), custom_call_target="tpu_custom_call" | custom-call | flops 536870912 | bytes 6291456 | tf_op jit(solution)/shard_map/pallas_call | solution.py:36
  19.8 0.8 copy-done.3
  20.6 0.9 shard_map.97
  21.5 10.9 %all-to-all-start.1 = ((bf16[16,144,128]{2,1,0:T(8,128)(2,1)}), bf16[16,144,128]{2,1,0:T(8,128)(2,1)S(1)}, u32[]{:S(2)}, u32[]{:S(2)}) async-start(bf16[16,144,128]{2,1,0:T(8,128)(2,1)} %get-tuple-element.20), calls=%async_computation.1 | async-start | bytes 1179648 | tf_op jit(solution)/shard_map/all_to_all | solution.py:252
  32.4 3.9 %collective-permute-start.3 = (bf16[32,4096]{1,0:T(8,128)(2,1)}, bf16[32,4096]{1,0:T(8,128)(2,1)S(1)}, u32[]{:S(2)}, u32[]{:S(2)}) collective-permute-start(bf16[32,4096]{1,0:T(8,128)(2,1)} %get-tuple-element.24), channel_id=1, source_target_pairs={{0,64},{64,128},{128,192},{192,0},{1,65},{65,129},{129,193},{193,1... | collective-permute-start | bytes 786440 | tf_op jit(solution)/shard_map/ppermute | solution.py:257
  36.4 4.6 %collective-permute-start.4 = (bf16[32,4096]{1,0:T(8,128)(2,1)}, bf16[32,4096]{1,0:T(8,128)(2,1)}, u32[]{:S(2)}, u32[]{:S(2)}) collective-permute-start(bf16[32,4096]{1,0:T(8,128)(2,1)} %get-tuple-element.25), channel_id=1, source_target_pairs={{0,128},{64,192},{128,0},{192,64},{1,129},{65,193},{129,1},{193,65... | collective-permute-start | bytes 786440 | tf_op jit(solution)/shard_map/ppermute | solution.py:257
  40.9 3.4 %collective-permute-start.5 = (bf16[32,4096]{1,0:T(8,128)(2,1)}, bf16[32,4096]{1,0:T(8,128)(2,1)}, u32[]{:S(2)}, u32[]{:S(2)}) collective-permute-start(bf16[32,4096]{1,0:T(8,128)(2,1)} %get-tuple-element.26), channel_id=1, source_target_pairs={{0,192},{64,0},{128,64},{192,128},{1,193},{65,1},{129,65},{193,129... | collective-permute-start | bytes 786440 | tf_op jit(solution)/shard_map/ppermute | solution.py:257
  44.3 6.1 %all-to-all-done.1.near_ref = bf16[16,144,128]{2,1,0:T(8,128)(2,1)S(1)} async-done(((bf16[16,144,128]{2,1,0:T(8,128)(2,1)}), bf16[16,144,128]{2,1,0:T(8,128)(2,1)S(1)}, u32[]{:S(2)}, u32[]{:S(2)}) %all-to-all-start.1) | async-done | bytes 589856 | tf_op jit(solution)/shard_map/all_to_all | solution.py:252
  50.4 3.3 %collective-permute-start.1 = (bf16[16,144,128]{2,1,0:T(8,128)(2,1)S(1)}, bf16[16,144,128]{2,1,0:T(8,128)(2,1)S(1)}, u32[]{:S(2)}, u32[]{:S(2)}) collective-permute-start(bf16[16,144,128]{2,1,0:T(8,128)(2,1)S(1)} %all-to-all-done.1.near_ref), channel_id=1, source_target_pairs={{0,304},{16,32},{32,16},{48,256},{256,48},{272,288},{288,272},{304... | collective-permute-start | bytes 1769480 | tf_op jit(solution)/shard_map/ppermute | solution.py:254
  53.7 1.0 %copy-done.4 = f32[32,4096]{1,0:T(8,128)S(1)} copy-done((f32[32,4096]{1,0:T(8,128)S(1)}, f32[32,4096]{1,0:T(8,128)}, u32[]{:S(2)}) %copy-start.4) | copy-done | bytes 524312
  54.8 1.3 %shard_map.99 = bf16[32,32,128]{2,1,0:T(8,128)(2,1)S(1)} custom-call(bf16[16,144,128]{2,1,0:T(8,128)(2,1)S(1)} %all-to-all-done.1.near_ref, f32[32,4096]{1,0:T(8,128)S(1)} %copy-done.4, bf16[32,4096]{1,0:T(8,128)(2,1)S(1)} %collective-permute-done.3.one_ref, bf16[32,4096]{1,0:T(8,128)(2,1)} %collective-permute-done.4.two_ref, ...), custom_call_target="tpu_custom_call" | custom-call | bytes 2097152 | tf_op jit(solution)/shard_map/pallas_call | solution.py:36
  56.0 0.7 copy-done.2
  56.7 8.7 %all-to-all-start.2 = ((bf16[32,32,128]{2,1,0:T(8,128)(2,1)}), bf16[32,32,128]{2,1,0:T(8,128)(2,1)S(1)}, u32[]{:S(2)}, u32[]{:S(2)}) async-start(bf16[32,32,128]{2,1,0:T(8,128)(2,1)} %copy-done.2), calls=%async_computation.2 | async-start | bytes 524288 | tf_op jit(solution)/shard_map/all_to_all | solution.py:269
  65.4 5.4 %collective-permute-done.1.far_ref = bf16[16,144,128]{2,1,0:T(8,128)(2,1)S(1)} collective-permute-done((bf16[16,144,128]{2,1,0:T(8,128)(2,1)S(1)}, bf16[16,144,128]{2,1,0:T(8,128)(2,1)S(1)}, u32[]{:S(2)}, u32[]{:S(2)}) %collective-permute-start.1) | collective-permute-done | bytes 589856 | tf_op jit(solution)/shard_map/ppermute | solution.py:254
  70.8 3.5 %shard_map.98 = (f32[256,128]{1,0:T(8,128)S(1)}, f32[256,128]{1,0:T(8,128)}) custom-call(bf16[16,144,128]{2,1,0:T(8,128)(2,1)S(1)} %all-to-all-done.1.near_ref, bf16[16,144,128]{2,1,0:T(8,128)(2,1)S(1)} %collective-permute-done.1.far_ref, bf16[256,4096]{1,0:T(8,128)(2,1)S(1)} %shard_map.94.own_ref, bf16[256,4224]{1,0:T(8,128)(2,1)} %collective-permute-done.other_ref), custom_call_target="tpu_custom_call" | custom-call | flops 536870912 | bytes 6291456 | tf_op jit(solution)/shard_map/pallas_call | solution.py:36
  74.3 0.6 copy-done.7
  75.0 1.9 %collective-permute-start.2 = (f32[256,128]{1,0:T(8,128)}, f32[256,128]{1,0:T(8,128)S(1)}, u32[]{:S(2)}, u32[]{:S(2)}) collective-permute-start(f32[256,128]{1,0:T(8,128)} %get-tuple-element.22), channel_id=1, source_target_pairs={{0,1},{1,0},{2,3},{3,2},{4,5},{5,4},{6,7},{7,6},{8,9},{9,8},{10,11... | collective-permute-start | bytes 393224 | tf_op jit(solution)/shard_map/ppermute | solution.py:278
  76.9 0.8 shard_map.100
  77.7 8.9 %all-to-all-start.3 = ((f32[8,40,128]{2,1,0:T(8,128)}), f32[8,40,128]{2,1,0:T(8,128)S(1)}, u32[]{:S(2)}, u32[]{:S(2)}) async-start(f32[8,40,128]{2,1,0:T(8,128)} %shard_map.100), calls=%async_computation.3 | async-start | bytes 327680 | tf_op jit(solution)/shard_map/all_to_all | solution.py:290
  86.5 1.6 %add_convert_fusion = bf16[256,128]{1,0:T(8,128)(2,1)} fusion(f32[256,128]{1,0:T(8,128)} %copy-done.7, f32[256,128]{1,0:T(8,128)S(1)} %collective-permute-done.2), kind=kLoop, calls=%fused_computation | loop fusion | flops 65536 | bytes 327680 | tf_op jit(solution)/shard_map/convert_element_type | solution.py:278
  88.1 9.2 %all-to-all-done.3.shares_ref = f32[8,40,128]{2,1,0:T(8,128)S(1)} async-done(((f32[8,40,128]{2,1,0:T(8,128)}), f32[8,40,128]{2,1,0:T(8,128)S(1)}, u32[]{:S(2)}, u32[]{:S(2)}) %all-to-all-start.3) | async-done | bytes 163872 | tf_op jit(solution)/shard_map/all_to_all | solution.py:290
  97.3 0.8 shard_map.101
  (22 shorter events, 0.0 us)
Async XLA Ops:
  0.6 2.2 %copy-start = (bf16[256,8192]{1,0:T(8,128)(2,1)S(1)}, bf16[256,8192]{1,0:T(8,128)(2,1)}, u32[]{:S(2)}) copy-start(bf16[256,8192]{1,0:T(8,128)(2,1)} %act_ref.3) | copy-start | bytes 12582916
  2.8 0.8 copy-start.5
  3.7 3.9 %copy-start.9 = (s32[16]{0:T(128)S(1)}, s32[16]{0:T(128)}, u32[]{:S(2)}) copy-start(s32[16]{0:T(128)} %prompt_ref.3) | copy-start | bytes 196
  3.7 3.9 %copy-start.10 = (f32[256]{0:T(256)S(1)}, f32[256]{0:T(256)}, u32[]{:S(2)}) copy-start(f32[256]{0:T(256)} %param.9) | copy-start | bytes 3076
  3.7 4.0 %copy-start.11 = (f32[256]{0:T(256)S(1)}, f32[256]{0:T(256)}, u32[]{:S(2)}) copy-start(f32[256]{0:T(256)} %param.10) | copy-start | bytes 3076
  5.7 10.3 %collective-permute-start = (bf16[256,4224]{1,0:T(8,128)(2,1)}, bf16[256,4224]{1,0:T(8,128)(2,1)}, u32[]{:S(2)}, u32[]{:S(2)}) collective-permute-start(bf16[256,4224]{1,0:T(8,128)(2,1)} %shard_map.95), channel_id=1, source_target_pairs={{0,1},{1,0},{2,3},{3,2},{4,5},{5,4},{6,7},{7,6},{8,9},{9,8},{10,11... | collective-permute-start | bytes 6488072 | tf_op jit(solution)/shard_map/ppermute | solution.py:228
  8.9 11.7 %all-to-all-start = ((f32[8,8,128]{2,1,0:T(8,128)}), f32[8,8,128]{2,1,0:T(8,128)S(1)}, u32[]{:S(2)}, u32[]{:S(2)}) async-start(f32[8,8,128]{2,1,0:T(8,128)} %shard_map.93.after_ref), calls=%async_computation | async-start | bytes 65536 | tf_op jit(solution)/shard_map/all_to_all | solution.py:207
  13.3 2.2 %copy-start.1 = (bf16[256,8192]{1,0:T(8,128)(2,1)S(1)}, bf16[256,8192]{1,0:T(8,128)(2,1)}, u32[]{:S(2)}) copy-start(bf16[256,8192]{1,0:T(8,128)(2,1)} %act_ref.3) | copy-start | bytes 12582916
  15.5 0.8 copy-start.6
  16.0 4.7 %copy-start.8 = (bf16[128,128]{1,0:T(8,128)(2,1)S(1)}, bf16[128,128]{1,0:T(8,128)(2,1)}, u32[]{:S(2)}) copy-start(bf16[128,128]{1,0:T(8,128)(2,1)} %weight_ref.1) | copy-start | bytes 98308
  19.8 0.8 copy-start.3
  21.5 28.9 %all-to-all-start.1 = ((bf16[16,144,128]{2,1,0:T(8,128)(2,1)}), bf16[16,144,128]{2,1,0:T(8,128)(2,1)S(1)}, u32[]{:S(2)}, u32[]{:S(2)}) async-start(bf16[16,144,128]{2,1,0:T(8,128)(2,1)} %get-tuple-element.20), calls=%async_computation.1 | async-start | bytes 1179648 | tf_op jit(solution)/shard_map/all_to_all | solution.py:252
  32.4 21.2 %collective-permute-start.3 = (bf16[32,4096]{1,0:T(8,128)(2,1)}, bf16[32,4096]{1,0:T(8,128)(2,1)S(1)}, u32[]{:S(2)}, u32[]{:S(2)}) collective-permute-start(bf16[32,4096]{1,0:T(8,128)(2,1)} %get-tuple-element.24), channel_id=1, source_target_pairs={{0,64},{64,128},{128,192},{192,0},{1,65},{65,129},{129,193},{193,1... | collective-permute-start | bytes 786440 | tf_op jit(solution)/shard_map/ppermute | solution.py:257
  36.4 17.3 %collective-permute-start.4 = (bf16[32,4096]{1,0:T(8,128)(2,1)}, bf16[32,4096]{1,0:T(8,128)(2,1)}, u32[]{:S(2)}, u32[]{:S(2)}) collective-permute-start(bf16[32,4096]{1,0:T(8,128)(2,1)} %get-tuple-element.25), channel_id=1, source_target_pairs={{0,128},{64,192},{128,0},{192,64},{1,129},{65,193},{129,1},{193,65... | collective-permute-start | bytes 786440 | tf_op jit(solution)/shard_map/ppermute | solution.py:257
  40.9 12.8 %collective-permute-start.5 = (bf16[32,4096]{1,0:T(8,128)(2,1)}, bf16[32,4096]{1,0:T(8,128)(2,1)}, u32[]{:S(2)}, u32[]{:S(2)}) collective-permute-start(bf16[32,4096]{1,0:T(8,128)(2,1)} %get-tuple-element.26), channel_id=1, source_target_pairs={{0,192},{64,0},{128,64},{192,128},{1,193},{65,1},{129,65},{193,129... | collective-permute-start | bytes 786440 | tf_op jit(solution)/shard_map/ppermute | solution.py:257
  50.4 20.4 %collective-permute-start.1 = (bf16[16,144,128]{2,1,0:T(8,128)(2,1)S(1)}, bf16[16,144,128]{2,1,0:T(8,128)(2,1)S(1)}, u32[]{:S(2)}, u32[]{:S(2)}) collective-permute-start(bf16[16,144,128]{2,1,0:T(8,128)(2,1)S(1)} %all-to-all-done.1.near_ref), channel_id=1, source_target_pairs={{0,304},{16,32},{32,16},{48,256},{256,48},{272,288},{288,272},{304... | collective-permute-start | bytes 1769480 | tf_op jit(solution)/shard_map/ppermute | solution.py:254
  53.7 1.0 %copy-start.4 = (f32[32,4096]{1,0:T(8,128)S(1)}, f32[32,4096]{1,0:T(8,128)}, u32[]{:S(2)}) copy-start(f32[32,4096]{1,0:T(8,128)} %copy-done.3) | copy-start | bytes 1572868
  56.0 0.7 copy-start.2
  56.7 20.2 %all-to-all-start.2 = ((bf16[32,32,128]{2,1,0:T(8,128)(2,1)}), bf16[32,32,128]{2,1,0:T(8,128)(2,1)S(1)}, u32[]{:S(2)}, u32[]{:S(2)}) async-start(bf16[32,32,128]{2,1,0:T(8,128)(2,1)} %copy-done.2), calls=%async_computation.2 | async-start | bytes 524288 | tf_op jit(solution)/shard_map/all_to_all | solution.py:269
  74.3 0.6 copy-start.7
  75.0 11.5 %collective-permute-start.2 = (f32[256,128]{1,0:T(8,128)}, f32[256,128]{1,0:T(8,128)S(1)}, u32[]{:S(2)}, u32[]{:S(2)}) collective-permute-start(f32[256,128]{1,0:T(8,128)} %get-tuple-element.22), channel_id=1, source_target_pairs={{0,1},{1,0},{2,3},{3,2},{4,5},{5,4},{6,7},{7,6},{8,9},{9,8},{10,11... | collective-permute-start | bytes 393224 | tf_op jit(solution)/shard_map/ppermute | solution.py:278
  77.7 19.6 %all-to-all-start.3 = ((f32[8,40,128]{2,1,0:T(8,128)}), f32[8,40,128]{2,1,0:T(8,128)S(1)}, u32[]{:S(2)}, u32[]{:S(2)}) async-start(f32[8,40,128]{2,1,0:T(8,128)} %shard_map.100), calls=%async_computation.3 | async-start | bytes 327680 | tf_op jit(solution)/shard_map/all_to_all | solution.py:290

commit v4 on v2

--- a/solution.py
+++ b/solution.py
@@ -18,6 +18,7 @@
 BLOCKS = HALF // HEAD
 XS, ZS = 4, 8
 SHARE = HEAD // XS
+LEAST = SHARE // 2
 NEAR = 2 * ZS
 
 SIZES = (("yh", 2), ("x", XS), ("yp", 2), ("yq", 2), ("z", ZS), ("c", 2))
@@ -130,7 +131,9 @@
         total = keep_ref[:, at]
         for ref in (one_ref, two_ref, three_ref):
             total = total + ref[:, at].astype(F32)
-        out_ref[block] = total.astype(BF16)
+        total = total.astype(BF16)
+        for yh in range(2):
+            out_ref[yh, block] = total[yh * LEAST : (yh + 1) * LEAST]
 
 
 def project_kernel(near_ref, far_ref, own_ref, other_ref, mine_ref, theirs_ref):
@@ -152,21 +155,21 @@
     row = lax.broadcasted_iota(jnp.int32, (8, HEAD), 0)
     tail = jnp.where(row == 0, margin_of(near_ref[...]), margin_of(far_ref[...]))
     for replica in range(2 * XS):
-        out_ref[replica, :SHARE] = total
-        out_ref[replica, SHARE:] = tail
+        out_ref[replica, :LEAST] = total
+        out_ref[replica, LEAST:] = tail
 
 
 def last_kernel(shares_ref, grad_ref, margins_ref, loss_ref):
-    parts = [shares_ref[x, :SHARE] + shares_ref[XS + x, :SHARE] for x in range(XS)]
+    parts = [shares_ref[yh * XS + x, :LEAST] for x in range(XS) for yh in range(2)]
     grad_ref[...] = jnp.concatenate(parts).T
     yp, yq = lax.axis_index("yp"), lax.axis_index("yq")
     lane = lax.broadcasted_iota(jnp.int32, (1, HEAD), 1)
     margins = jnp.zeros((1, HEAD), F32)
     for yh in range(2):
         for x in range(XS):
-            near = shares_ref[yh * XS + x, SHARE : SHARE + 1]
-            flipped = shares_ref[(1 - yh) * XS + x, SHARE + 1 : SHARE + 2]
-            straight = shares_ref[yh * XS + x, SHARE + 1 : SHARE + 2]
+            near = shares_ref[yh * XS + x, LEAST : LEAST + 1]
+            flipped = shares_ref[(1 - yh) * XS + x, LEAST + 1 : LEAST + 2]
+            straight = shares_ref[yh * XS + x, LEAST + 1 : LEAST + 2]
             far = jnp.where(yp == yq, flipped, straight)
             pair = (yh * XS + x) * 2
             margins = jnp.where(lane == pair + yp, near, margins)
@@ -228,8 +231,8 @@
         lax.ppermute(chunk, "x", [(i, (i + step) % XS) for i in range(XS)])
         for step, chunk in ((1, one), (2, two), (3, three))
     ]
-    summed = local(add_kernel, shape((BLOCKS, SHARE, HEAD), BF16), [VMEM] * 4, keep, *sent, moved=2 << 20)
-    terms = lax.all_to_all(summed.reshape(-1, HEAD), ("yp", "yq", "z"), 0, 0, tiled=True)
+    summed = local(add_kernel, shape((2, BLOCKS, LEAST, HEAD), BF16), [VMEM] * 4, keep, *sent, moved=2 << 20)
+    terms = lax.all_to_all(summed.reshape(-1, HEAD), ("yh", "yp", "yq", "z"), 0, 0, tiled=True)
 
     mine, theirs = local(
         project_kernel,
@@ -240,12 +243,12 @@
     )
     projected = (mine + lax.ppermute(theirs, "c", SWAP)).astype(BF16)
 
-    high = SHARE + 8
+    high = LEAST + 8
     joined = local(
         join_kernel,
         shape((2 * XS, high, HEAD), F32),
-        [whole((BLOCKS, SHARE, HEAD)), tile, tile],
-        terms.reshape(BLOCKS, SHARE, HEAD), near, far,
+        [whole((2 * BLOCKS, LEAST, HEAD)), tile, tile],
+        terms.reshape(2 * BLOCKS, LEAST, HEAD), near, far,
         moved=1 << 20,
         grid=(1,),
         out_specs=whole((2 * XS, high, HEAD)),

time: 101 us -> 103 us (1.020)
  the two profiles are of different devices: /device:TPU:8 before, /device:TPU:16 now
where the time goes in v4:
time: 103 us; the launch traced here: 102 us
  starting transfers between devices  35.3 us (34%)
  blocking collectives  30.2 us (29%)
  waiting for transfers between devices  22.4 us (22%)
  Pallas kernels  7.71 us (7%)
  local copies, waits for them, and re-layouts  5.32 us (5%)
    all_to_all x1, blocking collectives, body(): lax.all_to_all(packed.reshape(-1, HEAD), ('yq', 'z'), 0, 0, tiled=True)  30.2 us
    ppermute x3, starting transfers between devices, body(): lax.ppermute(chunk, 'x', [(i, (i + step) % XS) for i in range(XS)])  11.4 us
    all_to_all x1, waiting for transfers between devices, body(): lax.all_to_all(joined.reshape(-1, HEAD), DP, 0, 0, tiled=True)  9.69 us
    all_to_all x1, starting transfers between devices, body(): lax.all_to_all(summed.reshape(-1, HEAD), ('yh', 'yp', 'yq', 'z'), 0, 0, t...  8.79 us
    pallas_call x8, Pallas kernels, local(): pl.pallas_call(kernel, out_shape=out_shape, in_specs=in_specs, compiler_p...  7.71 us
    all_to_all x1, waiting for transfers between devices, body(): lax.all_to_all(summed.reshape(-1, HEAD), ('yh', 'yp', 'yq', 'z'), 0, 0, t...  7.29 us
    all_to_all x1, starting transfers between devices, body(): lax.all_to_all(joined.reshape(-1, HEAD), DP, 0, 0, tiled=True)  6.37 us
    unnamed x20, local copies, waits for them, and re-layouts  5.32 us
  transfers between devices with their start and end apart: 9, of which 5 were waited for; matrix products, arithmetic and copies ran while one was open for 1% of the time, Pallas kernels for 4%

profile of v4, /device:TPU:16, one launch (start us, length us, event | category | flops | bytes accessed | tf_op | source)
XLA Modules:
  0.0 102.3 jit_solution(7790252920132450278)
XLA Ops:
  0.6 2.2 %copy-done.2 = bf16[256,8192]{1,0:T(8,128)(2,1)S(1)} copy-done((bf16[256,8192]{1,0:T(8,128)(2,1)S(1)}, bf16[256,8192]{1,0:T(8,128)(2,1)}, u32[]{:S(2)}) %copy-start.2) | copy-done | bytes 4194328
  2.8 0.8 copy-done.4
  3.7 0.9 shard_map.95
  4.6 1.9 %collective-permute-start.2 = (bf16[256,4224]{1,0:T(8,128)(2,1)S(1)}, bf16[256,4224]{1,0:T(8,128)(2,1)S(1)}, u32[]{:S(2)}, u32[]{:S(2)}) collective-permute-start(bf16[256,4224]{1,0:T(8,128)(2,1)S(1)} %get-tuple-element.16), channel_id=1, source_target_pairs={{0,1},{1,0},{2,3},{3,2},{4,5},{5,4},{6,7},{7,6},{8,9},{9,8},{10,11... | collective-permute-start | bytes 6488072 | tf_op jit(solution)/shard_map/ppermute | solution.py:216
  6.5 0.7 shard_map.93.own_ref
  7.2 2.4 %collective-permute-start = (f32[8,128]{1,0:T(8,128)S(1)}, f32[8,128]{1,0:T(8,128)S(1)}, u32[]{:S(2)}, u32[]{:S(2)}) collective-permute-start(f32[8,128]{1,0:T(8,128)S(1)} %shard_map.93.own_ref), channel_id=1, source_target_pairs={{0,1},{1,0},{2,3},{3,2},{4,5},{5,4},{6,7},{7,6},{8,9},{9,8},{10,11... | collective-permute-start | bytes 12296 | tf_op jit(solution)/shard_map/ppermute | solution.py:190
  9.6 1.1 %collective-permute-done.other_ref = f32[8,128]{1,0:T(8,128)S(1)} collective-permute-done((f32[8,128]{1,0:T(8,128)S(1)}, f32[8,128]{1,0:T(8,128)S(1)}, u32[]{:S(2)}, u32[]{:S(2)}) %collective-permute-start) | collective-permute-done | bytes 4128 | tf_op jit(solution)/shard_map/ppermute | solution.py:190
  10.7 0.1 shard_map.94
  10.8 30.2 %all_to_all.21.near_ref = bf16[16,144,128]{2,1,0:T(8,128)(2,1)S(1)} all-to-all(bf16[16,144,128]{2,1,0:T(8,128)(2,1)S(1)} %shard_map.94), channel_id=1, replica_groups=mesh['yh'=2,'x'=4,'yp'=2,'yq'=2,'z'=8,'c'=2] {'yq','z'}, dimensions={0} | all-to-all | bytes 1179648 | tf_op jit(solution)/shard_map/all_to_all | solution.py:199
  41.0 0.0 collective-permute-done.2.other_ref
  41.0 1.6 %shard_map.97 = (f32[32,4096]{1,0:T(8,128)S(1)}, bf16[32,4096]{1,0:T(8,128)(2,1)S(1)}, bf16[32,4096]{1,0:T(8,128)(2,1)S(1)}, bf16[32,4096]{1,0:T(8,128)(2,1)S(1)}) custom-call(s32[16]{0:T(128)S(1)} %copy-done.7, bf16[16,144,128]{2,1,0:T(8,128)(2,1)S(1)} %all_to_all.21.near_ref, bf16[256,4096]{1,0:T(8,128)(2,1)S(1)} %get-tuple-element.15.own_ref, ...), custom_call_target="tpu_custom_call" | custom-call | flops 536870912 | bytes 6291456 | tf_op jit(solution)/shard_map/pallas_call | solution.py:36
  42.6 3.4 %collective-permute-start.4 = (bf16[32,4096]{1,0:T(8,128)(2,1)S(1)}, bf16[32,4096]{1,0:T(8,128)(2,1)S(1)}, u32[]{:S(2)}, u32[]{:S(2)}) collective-permute-start(bf16[32,4096]{1,0:T(8,128)(2,1)S(1)} %get-tuple-element.20), channel_id=1, source_target_pairs={{0,64},{64,128},{128,192},{192,0},{1,65},{65,129},{129,193},{193,1... | collective-permute-start | bytes 786440 | tf_op jit(solution)/shard_map/ppermute | solution.py:231
  46.0 4.6 %collective-permute-start.5 = (bf16[32,4096]{1,0:T(8,128)(2,1)S(1)}, bf16[32,4096]{1,0:T(8,128)(2,1)S(1)}, u32[]{:S(2)}, u32[]{:S(2)}) collective-permute-start(bf16[32,4096]{1,0:T(8,128)(2,1)S(1)} %get-tuple-element.21), channel_id=1, source_target_pairs={{0,128},{64,192},{128,0},{192,64},{1,129},{65,193},{129,1},{193,65... | collective-permute-start | bytes 786440 | tf_op jit(solution)/shard_map/ppermute | solution.py:231
  50.7 3.3 %collective-permute-start.6 = (bf16[32,4096]{1,0:T(8,128)(2,1)S(1)}, bf16[32,4096]{1,0:T(8,128)(2,1)S(1)}, u32[]{:S(2)}, u32[]{:S(2)}) collective-permute-start(bf16[32,4096]{1,0:T(8,128)(2,1)S(1)} %get-tuple-element.22), channel_id=1, source_target_pairs={{0,192},{64,0},{128,64},{192,128},{1,193},{65,1},{129,65},{193,129... | collective-permute-start | bytes 786440 | tf_op jit(solution)/shard_map/ppermute | solution.py:231
  54.0 2.5 %collective-permute-start.1 = (bf16[16,144,128]{2,1,0:T(8,128)(2,1)S(1)}, bf16[16,144,128]{2,1,0:T(8,128)(2,1)S(1)}, u32[]{:S(2)}, u32[]{:S(2)}) collective-permute-start(bf16[16,144,128]{2,1,0:T(8,128)(2,1)S(1)} %all_to_all.21.near_ref), channel_id=1, source_target_pairs={{0,304},{16,32},{32,16},{48,256},{256,48},{272,288},{288,272},{304... | collective-permute-start | bytes 1769480 | tf_op jit(solution)/shard_map/ppermute | solution.py:201
  56.5 0.0 collective-permute-done.4.one_ref
  56.5 2.8 %collective-permute-done.5.two_ref = bf16[32,4096]{1,0:T(8,128)(2,1)S(1)} collective-permute-done((bf16[32,4096]{1,0:T(8,128)(2,1)S(1)}, bf16[32,4096]{1,0:T(8,128)(2,1)S(1)}, u32[]{:S(2)}, u32[]{:S(2)}) %collective-permute-start.5) | collective-permute-done | bytes 262176 | tf_op jit(solution)/shard_map/ppermute | solution.py:231
  59.3 1.5 %collective-permute-done.6.three_ref = bf16[32,4096]{1,0:T(8,128)(2,1)S(1)} collective-permute-done((bf16[32,4096]{1,0:T(8,128)(2,1)S(1)}, bf16[32,4096]{1,0:T(8,128)(2,1)S(1)}, u32[]{:S(2)}, u32[]{:S(2)}) %collective-permute-start.6) | collective-permute-done | bytes 262176 | tf_op jit(solution)/shard_map/ppermute | solution.py:231
  60.8 0.1 shard_map.98
  60.9 0.7 copy-done.3
  61.6 8.8 %all-to-all-start.1 = ((bf16[64,16,128]{2,1,0:T(8,128)(2,1)}), bf16[64,16,128]{2,1,0:T(8,128)(2,1)}, u32[]{:S(2)}, u32[]{:S(2)}) async-start(bf16[64,16,128]{2,1,0:T(8,128)(2,1)} %bitcast.5), calls=%async_computation.1 | async-start | bytes 524288 | tf_op jit(solution)/shard_map/all_to_all | solution.py:235
  70.4 0.0 collective-permute-done.1.far_ref
  70.4 1.6 %copy-done.1 = bf16[256,4096]{1,0:T(8,128)(2,1)S(1)} copy-done((bf16[256,4096]{1,0:T(8,128)(2,1)S(1)}, bf16[256,4096]{1,0:T(8,128)(2,1)}, u32[]{:S(2)}) %copy-start.1) | copy-done | bytes 2097176
  72.0 1.9 %shard_map.96 = (f32[256,128]{1,0:T(8,128)S(1)}, f32[256,128]{1,0:T(8,128)}) custom-call(bf16[16,144,128]{2,1,0:T(8,128)(2,1)S(1)} %all_to_all.21.near_ref, bf16[16,144,128]{2,1,0:T(8,128)(2,1)S(1)} %collective-permute-done.1.far_ref, bf16[256,4096]{1,0:T(8,128)(2,1)S(1)} %copy-done.1, bf16[256,4224]{1,0:T(8,128)(2,1)S(1)} %collective-permute-done.2.other_ref), custom_call_target="tpu_custom_call" | custom-call | flops 536870912 | bytes 6291456 | tf_op jit(solution)/shard_map/pallas_call | solution.py:36
  73.9 1.9 %collective-permute-start.3 = (f32[256,128]{1,0:T(8,128)}, f32[256,128]{1,0:T(8,128)S(1)}, u32[]{:S(2)}, u32[]{:S(2)}) collective-permute-start(f32[256,128]{1,0:T(8,128)} %get-tuple-element.18), channel_id=1, source_target_pairs={{0,1},{1,0},{2,3},{3,2},{4,5},{5,4},{6,7},{7,6},{8,9},{9,8},{10,11... | collective-permute-start | bytes 393224 | tf_op jit(solution)/shard_map/ppermute | solution.py:244
  75.9 7.3 %all-to-all-done.1.terms_ref = bf16[64,16,128]{2,1,0:T(8,128)(2,1)} async-done(((bf16[64,16,128]{2,1,0:T(8,128)(2,1)}), bf16[64,16,128]{2,1,0:T(8,128)(2,1)}, u32[]{:S(2)}, u32[]{:S(2)}) %all-to-all-start.1) | async-done | bytes 262176 | tf_op jit(solution)/shard_map/all_to_all | solution.py:235
  83.1 1.7 %shard_map.99 = f32[8,24,128]{2,1,0:T(8,128)} custom-call(bf16[64,16,128]{2,1,0:T(8,128)(2,1)} %all-to-all-done.1.terms_ref, bf16[16,144,128]{2,1,0:T(8,128)(2,1)S(1)} %all_to_all.21.near_ref, bf16[16,144,128]{2,1,0:T(8,128)(2,1)S(1)} %collective-permute-done.1.far_ref), custom_call_target="tpu_custom_call" | custom-call | bytes 1048576 | tf_op jit(solution)/shard_map/pallas_call | solution.py:36
  84.8 6.4 %all-to-all-start.2 = ((f32[8,24,128]{2,1,0:T(8,128)}), f32[8,24,128]{2,1,0:T(8,128)S(1)}, u32[]{:S(2)}, u32[]{:S(2)}) async-start(f32[8,24,128]{2,1,0:T(8,128)} %shard_map.99), calls=%async_computation.2 | async-start | bytes 196608 | tf_op jit(solution)/shard_map/all_to_all | solution.py:256
  91.2 0.0 collective-permute-done.3
  91.2 0.6 add_convert_fusion
  91.8 9.7 %all-to-all-done.2.shares_ref = f32[8,24,128]{2,1,0:T(8,128)S(1)} async-done(((f32[8,24,128]{2,1,0:T(8,128)}), f32[8,24,128]{2,1,0:T(8,128)S(1)}, u32[]{:S(2)}, u32[]{:S(2)}) %all-to-all-start.2) | async-done | bytes 98336 | tf_op jit(solution)/shard_map/all_to_all | solution.py:256
  101.5 0.8 shard_map.100
  (16 shorter events, 0.0 us)
Async XLA Ops:
  0.6 2.2 %copy-start.2 = (bf16[256,8192]{1,0:T(8,128)(2,1)S(1)}, bf16[256,8192]{1,0:T(8,128)(2,1)}, u32[]{:S(2)}) copy-start(bf16[256,8192]{1,0:T(8,128)(2,1)} %act_ref.1) | copy-start | bytes 12582916
  2.8 0.8 copy-start.4
  3.7 2.9 %copy-start.7 = (s32[16]{0:T(128)S(1)}, s32[16]{0:T(128)}, u32[]{:S(2)}) copy-start(s32[16]{0:T(128)} %prompt_ref.3) | copy-start | bytes 196
  3.7 2.9 %copy-start.8 = (f32[256]{0:T(256)S(1)}, f32[256]{0:T(256)}, u32[]{:S(2)}) copy-start(f32[256]{0:T(256)} %param.9) | copy-start | bytes 3076
  3.7 2.9 %copy-start.9 = (f32[256]{0:T(256)S(1)}, f32[256]{0:T(256)}, u32[]{:S(2)}) copy-start(f32[256]{0:T(256)} %param.10) | copy-start | bytes 3076
  3.7 7.1 %copy-start.6 = (bf16[128,128]{1,0:T(8,128)(2,1)S(1)}, bf16[128,128]{1,0:T(8,128)(2,1)}, u32[]{:S(2)}) copy-start(bf16[128,128]{1,0:T(8,128)(2,1)} %weight_ref.1) | copy-start | bytes 98308
  3.7 37.4 %copy-start.5 = (bf16[256,128]{1,0:T(8,128)(2,1)S(1)}, bf16[256,128]{1,0:T(8,128)(2,1)}, u32[]{:S(2)}) copy-start(bf16[256,128]{1,0:T(8,128)(2,1)} %sens_ref.3) | copy-start | bytes 196612
  4.6 38.0 %copy-start = (bf16[256,4096]{1,0:T(8,128)(2,1)}, bf16[256,4096]{1,0:T(8,128)(2,1)S(1)}, u32[]{:S(2)}) copy-start(bf16[256,4096]{1,0:T(8,128)(2,1)S(1)} %get-tuple-element.15.own_ref) | copy-start | bytes 6291460
  4.6 36.4 %collective-permute-start.2 = (bf16[256,4224]{1,0:T(8,128)(2,1)S(1)}, bf16[256,4224]{1,0:T(8,128)(2,1)S(1)}, u32[]{:S(2)}, u32[]{:S(2)}) collective-permute-start(bf16[256,4224]{1,0:T(8,128)(2,1)S(1)} %get-tuple-element.16), channel_id=1, source_target_pairs={{0,1},{1,0},{2,3},{3,2},{4,5},{5,4},{6,7},{7,6},{8,9},{9,8},{10,11... | collective-permute-start | bytes 6488072 | tf_op jit(solution)/shard_map/ppermute | solution.py:216
  7.2 3.5 %collective-permute-start = (f32[8,128]{1,0:T(8,128)S(1)}, f32[8,128]{1,0:T(8,128)S(1)}, u32[]{:S(2)}, u32[]{:S(2)}) collective-permute-start(f32[8,128]{1,0:T(8,128)S(1)} %shard_map.93.own_ref), channel_id=1, source_target_pairs={{0,1},{1,0},{2,3},{3,2},{4,5},{5,4},{6,7},{7,6},{8,9},{9,8},{10,11... | collective-permute-start | bytes 12296 | tf_op jit(solution)/shard_map/ppermute | solution.py:190
  42.6 13.9 %collective-permute-start.4 = (bf16[32,4096]{1,0:T(8,128)(2,1)S(1)}, bf16[32,4096]{1,0:T(8,128)(2,1)S(1)}, u32[]{:S(2)}, u32[]{:S(2)}) collective-permute-start(bf16[32,4096]{1,0:T(8,128)(2,1)S(1)} %get-tuple-element.20), channel_id=1, source_target_pairs={{0,64},{64,128},{128,192},{192,0},{1,65},{65,129},{129,193},{193,1... | collective-permute-start | bytes 786440 | tf_op jit(solution)/shard_map/ppermute | solution.py:231
  46.0 13.3 %collective-permute-start.5 = (bf16[32,4096]{1,0:T(8,128)(2,1)S(1)}, bf16[32,4096]{1,0:T(8,128)(2,1)S(1)}, u32[]{:S(2)}, u32[]{:S(2)}) collective-permute-start(bf16[32,4096]{1,0:T(8,128)(2,1)S(1)} %get-tuple-element.21), channel_id=1, source_target_pairs={{0,128},{64,192},{128,0},{192,64},{1,129},{65,193},{129,1},{193,65... | collective-permute-start | bytes 786440 | tf_op jit(solution)/shard_map/ppermute | solution.py:231
  50.7 10.1 %collective-permute-start.6 = (bf16[32,4096]{1,0:T(8,128)(2,1)S(1)}, bf16[32,4096]{1,0:T(8,128)(2,1)S(1)}, u32[]{:S(2)}, u32[]{:S(2)}) collective-permute-start(bf16[32,4096]{1,0:T(8,128)(2,1)S(1)} %get-tuple-element.22), channel_id=1, source_target_pairs={{0,192},{64,0},{128,64},{192,128},{1,193},{65,1},{129,65},{193,129... | collective-permute-start | bytes 786440 | tf_op jit(solution)/shard_map/ppermute | solution.py:231
  54.0 16.4 %collective-permute-start.1 = (bf16[16,144,128]{2,1,0:T(8,128)(2,1)S(1)}, bf16[16,144,128]{2,1,0:T(8,128)(2,1)S(1)}, u32[]{:S(2)}, u32[]{:S(2)}) collective-permute-start(bf16[16,144,128]{2,1,0:T(8,128)(2,1)S(1)} %all_to_all.21.near_ref), channel_id=1, source_target_pairs={{0,304},{16,32},{32,16},{48,256},{256,48},{272,288},{288,272},{304... | collective-permute-start | bytes 1769480 | tf_op jit(solution)/shard_map/ppermute | solution.py:201
  60.9 0.7 copy-start.3
  61.6 21.5 %all-to-all-start.1 = ((bf16[64,16,128]{2,1,0:T(8,128)(2,1)}), bf16[64,16,128]{2,1,0:T(8,128)(2,1)}, u32[]{:S(2)}, u32[]{:S(2)}) async-start(bf16[64,16,128]{2,1,0:T(8,128)(2,1)} %bitcast.5), calls=%async_computation.1 | async-start | bytes 524288 | tf_op jit(solution)/shard_map/all_to_all | solution.py:235
  70.4 1.6 %copy-start.1 = (bf16[256,4096]{1,0:T(8,128)(2,1)S(1)}, bf16[256,4096]{1,0:T(8,128)(2,1)}, u32[]{:S(2)}) copy-start(bf16[256,4096]{1,0:T(8,128)(2,1)} %copy-done) | copy-start | bytes 6291460
  73.9 17.3 %collective-permute-start.3 = (f32[256,128]{1,0:T(8,128)}, f32[256,128]{1,0:T(8,128)S(1)}, u32[]{:S(2)}, u32[]{:S(2)}) collective-permute-start(f32[256,128]{1,0:T(8,128)} %get-tuple-element.18), channel_id=1, source_target_pairs={{0,1},{1,0},{2,3},{3,2},{4,5},{5,4},{6,7},{7,6},{8,9},{9,8},{10,11... | collective-permute-start | bytes 393224 | tf_op jit(solution)/shard_map/ppermute | solution.py:244
  84.8 16.7 %all-to-all-start.2 = ((f32[8,24,128]{2,1,0:T(8,128)}), f32[8,24,128]{2,1,0:T(8,128)S(1)}, u32[]{:S(2)}, u32[]{:S(2)}) async-start(f32[8,24,128]{2,1,0:T(8,128)} %shard_map.99), calls=%async_computation.2 | async-start | bytes 196608 | tf_op jit(solution)/shard_map/all_to_all | solution.py:256

commit v5 on v3

--- a/solution.py
+++ b/solution.py
@@ -78,24 +78,18 @@
         out_ref[chip, HEAD:] = tile.astype(BF16)
 
 
-def columns_of(act_ref, out_ref, index):
+def split_kernel(act_ref, sens_ref, own_ref, send_ref):
     def move(parity):
         for block in range(BLOCKS):
-            start = (2 * block + parity) * HEAD
-            out_ref[:, block * HEAD : (block + 1) * HEAD] = act_ref[:, start : start + HEAD]
-
-    pl.when(index == 0)(lambda: move(0))
-    pl.when(index == 1)(lambda: move(1))
-
-
-def send_kernel(act_ref, sens_ref, out_ref):
-    columns_of(act_ref, out_ref, 1 - lax.axis_index("c"))
-    out_ref[:, HALF:] = sens_ref[...]
-
-
-def own_kernel(act_ref, after_ref, out_ref):
-    del after_ref
-    columns_of(act_ref, out_ref, lax.axis_index("c"))
+            to = slice(block * HEAD, (block + 1) * HEAD)
+            mine, theirs = (2 * block + parity) * HEAD, (2 * block + 1 - parity) * HEAD
+            own_ref[:, to] = act_ref[:, mine : mine + HEAD]
+            send_ref[:, to] = act_ref[:, theirs : theirs + HEAD]
+
+    core = lax.axis_index("c")
+    pl.when(core == 0)(lambda: move(0))
+    pl.when(core == 1)(lambda: move(1))
+    send_ref[:, HALF:] = sens_ref[...]
 
 
 def margins_of(tiles):
@@ -206,24 +200,17 @@
     )
     parts = lax.all_to_all(part.reshape(-1, HEAD), ("x", "c"), 0, 0, tiled=True).reshape(2 * XS, 8, HEAD)
     strip = ROWS // 4
-    rows_of = lambda width: pl.BlockSpec((strip, width), lambda i: (i, 0))
-    send = local(
-        send_kernel,
-        shape((ROWS, HALF + HEAD), BF16),
-        [rows_of(WIDTH), rows_of(HEAD)],
+    own, send = local(
+        split_kernel,
+        (shape((ROWS, HALF), BF16), shape((ROWS, HALF + HEAD), BF16)),
+        [pl.BlockSpec((strip, WIDTH), lambda i: (i, 0)), pl.BlockSpec((strip, HEAD), lambda i: (i, 0))],
         activations, sensitivity,
-        moved=6 << 20,
+        moved=8 << 20,
         grid=(4,),
-        out_specs=rows_of(HALF + HEAD),
-    )
-    own = local(
-        own_kernel,
-        shape((ROWS, HALF), BF16),
-        [rows_of(WIDTH), ANY],
-        activations, part,
-        moved=6 << 20,
-        grid=(4,),
-        out_specs=rows_of(HALF),
+        out_specs=(
+            pl.BlockSpec((strip, HALF), lambda i: (i, 0)),
+            pl.BlockSpec((strip, HALF + HEAD), lambda i: (i, 0)),
+        ),
     )
     other = lax.ppermute(send, "c", SWAP)
 

time: 99 us -> 99 us (level)
  Pallas kernels: 14.5 us -> 12.7 us
  local copies, waits for them, and re-layouts: 8.75 us -> 10.1 us
    ppermute x1, waiting for transfers between devices: 5.39 us -> 3 us  [body(): far = lax.ppermute(near, ('yh', 'yp', 'yq'), outside)]
    pallas_call x9 -> x8, Pallas kernels: 14.5 us -> 12.7 us  [local(): pl.pallas_call(kernel, out_shape=out_shape, in_specs=in_specs, compiler_p...]
    all_to_all x1, waiting for transfers between devices: 9.23 us -> 10.8 us  [body(): lax.all_to_all(joined.reshape(-1, HEAD), DP, 0, 0, tiled=True)]
    all_to_all x1, waiting for transfers between devices: 0.01 us -> 1.48 us  [body(): lax.all_to_all(summed.reshape(-1, HEAD), ('yp', 'yq', 'z'), 0, 0, tiled=T...]
    unnamed x24 -> x26, local copies, waits for them, and re-layouts: 8.75 us -> 10.1 us
  transfers between devices with their start and end apart: 10 -> 10, of which waited for: 3 -> 5; matrix products, arithmetic and copies ran while one was open for 2% -> 1% of each run, Pallas kernels for 11% -> 9%
where the time goes in v5:
time: 99 us; the launch traced here: 98.2 us
  starting transfers between devices  52.7 us (53%)
  waiting for transfers between devices  21.3 us (22%)
  Pallas kernels  12.7 us (13%)
  local copies, waits for them, and re-layouts  10.1 us (10%)
    pallas_call x8, Pallas kernels, local(): pl.pallas_call(kernel, out_shape=out_shape, in_specs=in_specs, compiler_p...  12.7 us
    ppermute x3, starting transfers between devices, body(): lax.ppermute(chunk, 'x', [(i, (i + step) % XS) for i in range(XS)])  11.3 us
    all_to_all x1, starting transfers between devices, body(): lax.all_to_all(packed.reshape(-1, HEAD), ('yq', 'z'), 0, 0, tiled=True)  10.9 us
    all_to_all x1, waiting for transfers between devices, body(): lax.all_to_all(joined.reshape(-1, HEAD), DP, 0, 0, tiled=True)  10.8 us
    unnamed x26, local copies, waits for them, and re-layouts  10.1 us
    all_to_all x1, starting transfers between devices, body(): lax.all_to_all(joined.reshape(-1, HEAD), DP, 0, 0, tiled=True)  9.63 us
    all_to_all x1, starting transfers between devices, body(): lax.all_to_all(summed.reshape(-1, HEAD), ('yp', 'yq', 'z'), 0, 0, tiled=T...  8.97 us
    all_to_all x1, waiting for transfers between devices, body(): lax.all_to_all(packed.reshape(-1, HEAD), ('yq', 'z'), 0, 0, tiled=True)  5.42 us
  transfers between devices with their start and end apart: 10, of which 5 were waited for; matrix products, arithmetic and copies ran while one was open for 1% of the time, Pallas kernels for 9%

profile of v5, /device:TPU:72, one launch (start us, length us, event | category | flops | bytes accessed | tf_op | source)
XLA Modules:
  0.0 98.2 jit_solution(14402449083549115102)
XLA Ops:
  0.6 2.2 %copy-done.3 = bf16[256,8192]{1,0:T(8,128)(2,1)S(1)} copy-done((bf16[256,8192]{1,0:T(8,128)(2,1)S(1)}, bf16[256,8192]{1,0:T(8,128)(2,1)}, u32[]{:S(2)}) %copy-start.3) | copy-done | bytes 4194328
  2.8 0.8 copy-done.7
  3.7 2.3 %shard_map.94 = (bf16[256,4096]{1,0:T(8,128)(2,1)S(1)}, bf16[256,4224]{1,0:T(8,128)(2,1)}) custom-call(bf16[256,8192]{1,0:T(8,128)(2,1)S(1)} %copy-done.3, bf16[256,128]{1,0:T(8,128)(2,1)S(1)} %copy-done.7), custom_call_target="tpu_custom_call" | custom-call | bytes 8388608 | tf_op jit(solution)/shard_map/pallas_call | solution.py:36
  5.9 1.3 %copy-done = bf16[256,4096]{1,0:T(8,128)(2,1)} copy-done((bf16[256,4096]{1,0:T(8,128)(2,1)}, bf16[256,4096]{1,0:T(8,128)(2,1)S(1)}, u32[]{:S(2)}) %copy-start) | copy-done | bytes 2097176
  7.3 1.9 %collective-permute-start = (bf16[256,4224]{1,0:T(8,128)(2,1)}, bf16[256,4224]{1,0:T(8,128)(2,1)S(1)}, u32[]{:S(2)}, u32[]{:S(2)}) collective-permute-start(bf16[256,4224]{1,0:T(8,128)(2,1)} %get-tuple-element.20), channel_id=1, source_target_pairs={{0,1},{1,0},{2,3},{3,2},{4,5},{5,4},{6,7},{7,6},{8,9},{9,8},{10,11... | collective-permute-start | bytes 6488072 | tf_op jit(solution)/shard_map/ppermute | solution.py:215
  9.2 1.3 %shard_map.93 = f32[8,8,128]{2,1,0:T(8,128)} custom-call(s32[16]{0:T(128)S(1)} %copy-done.10, f32[2,128]{1,0:T(2,128)S(1)} %bitcast.4, f32[2,128]{1,0:T(2,128)S(1)} %bitcast.5), custom_call_target="tpu_custom_call" | custom-call | bytes 40960 | tf_op jit(solution)/shard_map/pallas_call | solution.py:36
  10.5 4.4 %all-to-all-start = ((f32[8,8,128]{2,1,0:T(8,128)}), f32[8,8,128]{2,1,0:T(8,128)S(1)}, u32[]{:S(2)}, u32[]{:S(2)}) async-start(f32[8,8,128]{2,1,0:T(8,128)} %shard_map.93), calls=%async_computation | async-start | bytes 65536 | tf_op jit(solution)/shard_map/all_to_all | solution.py:201
  14.9 1.6 %copy-done.1 = bf16[256,4096]{1,0:T(8,128)(2,1)S(1)} copy-done((bf16[256,4096]{1,0:T(8,128)(2,1)S(1)}, bf16[256,4096]{1,0:T(8,128)(2,1)}, u32[]{:S(2)}) %copy-start.1) | copy-done | bytes 2097176
  16.5 2.4 %shard_map.95 = (f32[32,4096]{1,0:T(8,128)S(1)}, bf16[32,4096]{1,0:T(8,128)(2,1)}, bf16[32,4096]{1,0:T(8,128)(2,1)}, bf16[32,4096]{1,0:T(8,128)(2,1)}) custom-call(s32[16]{0:T(128)S(1)} %copy-done.10, bf16[256,4096]{1,0:T(8,128)(2,1)S(1)} %copy-done.1, bf16[256,4224]{1,0:T(8,128)(2,1)S(1)} %collective-permute-done.other_ref, bf16[256,128]{1,0:T(8,128)(2,1)S(1)} %copy-done.8), custom_call_target="tpu_custom_call" | custom-call | flops 536870912 | bytes 6291456 | tf_op jit(solution)/shard_map/pallas_call | solution.py:36
  19.0 0.8 copy-done.5
  19.8 0.6 all-to-all-done.parts_ref
  20.4 0.9 shard_map.96
  21.3 10.9 %all-to-all-start.1 = ((bf16[16,144,128]{2,1,0:T(8,128)(2,1)}), bf16[16,144,128]{2,1,0:T(8,128)(2,1)S(1)}, u32[]{:S(2)}, u32[]{:S(2)}) async-start(bf16[16,144,128]{2,1,0:T(8,128)(2,1)} %get-tuple-element.24), calls=%async_computation.1 | async-start | bytes 1179648 | tf_op jit(solution)/shard_map/all_to_all | solution.py:239
  32.1 3.3 %collective-permute-start.3 = (bf16[32,4096]{1,0:T(8,128)(2,1)}, bf16[32,4096]{1,0:T(8,128)(2,1)}, u32[]{:S(2)}, u32[]{:S(2)}) collective-permute-start(bf16[32,4096]{1,0:T(8,128)(2,1)} %get-tuple-element.28), channel_id=1, source_target_pairs={{0,64},{64,128},{128,192},{192,0},{1,65},{65,129},{129,193},{193,1... | collective-permute-start | bytes 786440 | tf_op jit(solution)/shard_map/ppermute | solution.py:244
  35.5 4.6 %collective-permute-start.4 = (bf16[32,4096]{1,0:T(8,128)(2,1)}, bf16[32,4096]{1,0:T(8,128)(2,1)}, u32[]{:S(2)}, u32[]{:S(2)}) collective-permute-start(bf16[32,4096]{1,0:T(8,128)(2,1)} %get-tuple-element.29), channel_id=1, source_target_pairs={{0,128},{64,192},{128,0},{192,64},{1,129},{65,193},{129,1},{193,65... | collective-permute-start | bytes 786440 | tf_op jit(solution)/shard_map/ppermute | solution.py:244
  40.1 3.4 %collective-permute-start.5 = (bf16[32,4096]{1,0:T(8,128)(2,1)}, bf16[32,4096]{1,0:T(8,128)(2,1)}, u32[]{:S(2)}, u32[]{:S(2)}) collective-permute-start(bf16[32,4096]{1,0:T(8,128)(2,1)} %get-tuple-element.30), channel_id=1, source_target_pairs={{0,192},{64,0},{128,64},{192,128},{1,193},{65,1},{129,65},{193,129... | collective-permute-start | bytes 786440 | tf_op jit(solution)/shard_map/ppermute | solution.py:244
  43.5 5.4 %all-to-all-done.1.near_ref = bf16[16,144,128]{2,1,0:T(8,128)(2,1)S(1)} async-done(((bf16[16,144,128]{2,1,0:T(8,128)(2,1)}), bf16[16,144,128]{2,1,0:T(8,128)(2,1)S(1)}, u32[]{:S(2)}, u32[]{:S(2)}) %all-to-all-start.1) | async-done | bytes 589856 | tf_op jit(solution)/shard_map/all_to_all | solution.py:239
  48.9 3.7 %collective-permute-start.1 = (bf16[16,144,128]{2,1,0:T(8,128)(2,1)S(1)}, bf16[16,144,128]{2,1,0:T(8,128)(2,1)S(1)}, u32[]{:S(2)}, u32[]{:S(2)}) collective-permute-start(bf16[16,144,128]{2,1,0:T(8,128)(2,1)S(1)} %all-to-all-done.1.near_ref), channel_id=1, source_target_pairs={{0,304},{16,32},{32,16},{48,256},{256,48},{272,288},{288,272},{304... | collective-permute-start | bytes 1769480 | tf_op jit(solution)/shard_map/ppermute | solution.py:241
  52.6 1.0 %copy-done.6 = f32[32,4096]{1,0:T(8,128)S(1)} copy-done((f32[32,4096]{1,0:T(8,128)S(1)}, f32[32,4096]{1,0:T(8,128)}, u32[]{:S(2)}) %copy-start.6) | copy-done | bytes 524312
  53.7 1.3 %shard_map.98 = bf16[32,32,128]{2,1,0:T(8,128)(2,1)S(1)} custom-call(bf16[16,144,128]{2,1,0:T(8,128)(2,1)S(1)} %all-to-all-done.1.near_ref, f32[32,4096]{1,0:T(8,128)S(1)} %copy-done.6, bf16[32,4096]{1,0:T(8,128)(2,1)} %collective-permute-done.3.one_ref, bf16[32,4096]{1,0:T(8,128)(2,1)} %collective-permute-done.4.two_ref, ...), custom_call_target="tpu_custom_call" | custom-call | bytes 2097152 | tf_op jit(solution)/shard_map/pallas_call | solution.py:36
  55.0 0.7 copy-done.4
  55.7 9.0 %all-to-all-start.2 = ((bf16[32,32,128]{2,1,0:T(8,128)(2,1)}), bf16[32,32,128]{2,1,0:T(8,128)(2,1)}, u32[]{:S(2)}, u32[]{:S(2)}) async-start(bf16[32,32,128]{2,1,0:T(8,128)(2,1)} %copy-done.4), calls=%async_computation.2 | async-start | bytes 524288 | tf_op jit(solution)/shard_map/all_to_all | solution.py:256
  64.7 3.0 %collective-permute-done.1.far_ref = bf16[16,144,128]{2,1,0:T(8,128)(2,1)S(1)} collective-permute-done((bf16[16,144,128]{2,1,0:T(8,128)(2,1)S(1)}, bf16[16,144,128]{2,1,0:T(8,128)(2,1)S(1)}, u32[]{:S(2)}, u32[]{:S(2)}) %collective-permute-start.1) | collective-permute-done | bytes 589856 | tf_op jit(solution)/shard_map/ppermute | solution.py:241
  67.7 1.6 %copy-done.2 = bf16[256,4096]{1,0:T(8,128)(2,1)S(1)} copy-done((bf16[256,4096]{1,0:T(8,128)(2,1)S(1)}, bf16[256,4096]{1,0:T(8,128)(2,1)}, u32[]{:S(2)}) %copy-start.2) | copy-done | bytes 2097176
  69.3 1.9 %shard_map.97 = (f32[256,128]{1,0:T(8,128)S(1)}, f32[256,128]{1,0:T(8,128)}) custom-call(bf16[16,144,128]{2,1,0:T(8,128)(2,1)S(1)} %all-to-all-done.1.near_ref, bf16[16,144,128]{2,1,0:T(8,128)(2,1)S(1)} %collective-permute-done.1.far_ref, bf16[256,4096]{1,0:T(8,128)(2,1)S(1)} %copy-done.2, bf16[256,4224]{1,0:T(8,128)(2,1)S(1)} %collective-permute-done.other_ref), custom_call_target="tpu_custom_call" | custom-call | flops 536870912 | bytes 6291456 | tf_op jit(solution)/shard_map/pallas_call | solution.py:36
  71.2 1.9 %collective-permute-start.2 = (f32[256,128]{1,0:T(8,128)}, f32[256,128]{1,0:T(8,128)S(1)}, u32[]{:S(2)}, u32[]{:S(2)}) collective-permute-start(f32[256,128]{1,0:T(8,128)} %get-tuple-element.26), channel_id=1, source_target_pairs={{0,1},{1,0},{2,3},{3,2},{4,5},{5,4},{6,7},{7,6},{8,9},{9,8},{10,11... | collective-permute-start | bytes 393224 | tf_op jit(solution)/shard_map/ppermute | solution.py:265
  73.1 1.5 %all-to-all-done.2.terms_ref = bf16[32,32,128]{2,1,0:T(8,128)(2,1)} async-done(((bf16[32,32,128]{2,1,0:T(8,128)(2,1)}), bf16[32,32,128]{2,1,0:T(8,128)(2,1)}, u32[]{:S(2)}, u32[]{:S(2)}) %all-to-all-start.2) | async-done | bytes 262176 | tf_op jit(solution)/shard_map/all_to_all | solution.py:256
  74.6 1.7 %shard_map.99 = f32[8,40,128]{2,1,0:T(8,128)} custom-call(bf16[32,32,128]{2,1,0:T(8,128)(2,1)} %all-to-all-done.2.terms_ref, bf16[16,144,128]{2,1,0:T(8,128)(2,1)S(1)} %all-to-all-done.1.near_ref, bf16[16,144,128]{2,1,0:T(8,128)(2,1)S(1)} %collective-permute-done.1.far_ref), custom_call_target="tpu_custom_call" | custom-call | bytes 1048576 | tf_op jit(solution)/shard_map/pallas_call | solution.py:36
  76.3 9.6 %all-to-all-start.3 = ((f32[8,40,128]{2,1,0:T(8,128)}), f32[8,40,128]{2,1,0:T(8,128)S(1)}, u32[]{:S(2)}, u32[]{:S(2)}) async-start(f32[8,40,128]{2,1,0:T(8,128)} %shard_map.99), calls=%async_computation.3 | async-start | bytes 327680 | tf_op jit(solution)/shard_map/all_to_all | solution.py:277
  85.9 0.6 add_convert_fusion
  86.6 10.8 %all-to-all-done.3.shares_ref = f32[8,40,128]{2,1,0:T(8,128)S(1)} async-done(((f32[8,40,128]{2,1,0:T(8,128)}), f32[8,40,128]{2,1,0:T(8,128)S(1)}, u32[]{:S(2)}, u32[]{:S(2)}) %all-to-all-start.3) | async-done | bytes 163872 | tf_op jit(solution)/shard_map/all_to_all | solution.py:277
  97.4 0.8 shard_map.100
  (23 shorter events, 0.0 us)
Async XLA Ops:
  0.6 2.2 %copy-start.3 = (bf16[256,8192]{1,0:T(8,128)(2,1)S(1)}, bf16[256,8192]{1,0:T(8,128)(2,1)}, u32[]{:S(2)}) copy-start(bf16[256,8192]{1,0:T(8,128)(2,1)} %act_ref.1) | copy-start | bytes 12582916
  2.8 0.8 copy-start.7
  3.7 5.5 %copy-start.10 = (s32[16]{0:T(128)S(1)}, s32[16]{0:T(128)}, u32[]{:S(2)}) copy-start(s32[16]{0:T(128)} %prompt_ref.3) | copy-start | bytes 196
  3.7 5.5 %copy-start.11 = (f32[256]{0:T(256)S(1)}, f32[256]{0:T(256)}, u32[]{:S(2)}) copy-start(f32[256]{0:T(256)} %param.9) | copy-start | bytes 3076
  3.7 5.5 %copy-start.12 = (f32[256]{0:T(256)S(1)}, f32[256]{0:T(256)}, u32[]{:S(2)}) copy-start(f32[256]{0:T(256)} %param.10) | copy-start | bytes 3076
  3.7 11.3 %copy-start.8 = (bf16[256,128]{1,0:T(8,128)(2,1)S(1)}, bf16[256,128]{1,0:T(8,128)(2,1)}, u32[]{:S(2)}) copy-start(bf16[256,128]{1,0:T(8,128)(2,1)} %sens_ref.3) | copy-start | bytes 196612
  5.9 1.3 %copy-start = (bf16[256,4096]{1,0:T(8,128)(2,1)}, bf16[256,4096]{1,0:T(8,128)(2,1)S(1)}, u32[]{:S(2)}) copy-start(bf16[256,4096]{1,0:T(8,128)(2,1)S(1)} %get-tuple-element.19.own_ref) | copy-start | bytes 6291460
  7.3 7.6 %collective-permute-start = (bf16[256,4224]{1,0:T(8,128)(2,1)}, bf16[256,4224]{1,0:T(8,128)(2,1)S(1)}, u32[]{:S(2)}, u32[]{:S(2)}) collective-permute-start(bf16[256,4224]{1,0:T(8,128)(2,1)} %get-tuple-element.20), channel_id=1, source_target_pairs={{0,1},{1,0},{2,3},{3,2},{4,5},{5,4},{6,7},{7,6},{8,9},{9,8},{10,11... | collective-permute-start | bytes 6488072 | tf_op jit(solution)/shard_map/ppermute | solution.py:215
  10.5 9.9 %all-to-all-start = ((f32[8,8,128]{2,1,0:T(8,128)}), f32[8,8,128]{2,1,0:T(8,128)S(1)}, u32[]{:S(2)}, u32[]{:S(2)}) async-start(f32[8,8,128]{2,1,0:T(8,128)} %shard_map.93), calls=%async_computation | async-start | bytes 65536 | tf_op jit(solution)/shard_map/all_to_all | solution.py:201
  14.9 1.6 %copy-start.1 = (bf16[256,4096]{1,0:T(8,128)(2,1)S(1)}, bf16[256,4096]{1,0:T(8,128)(2,1)}, u32[]{:S(2)}) copy-start(bf16[256,4096]{1,0:T(8,128)(2,1)} %copy-done) | copy-start | bytes 6291460
  16.5 3.8 %copy-start.9 = (bf16[128,128]{1,0:T(8,128)(2,1)S(1)}, bf16[128,128]{1,0:T(8,128)(2,1)}, u32[]{:S(2)}) copy-start(bf16[128,128]{1,0:T(8,128)(2,1)} %weight_ref.1) | copy-start | bytes 98308
  19.0 0.8 copy-start.5
  21.3 27.6 %all-to-all-start.1 = ((bf16[16,144,128]{2,1,0:T(8,128)(2,1)}), bf16[16,144,128]{2,1,0:T(8,128)(2,1)S(1)}, u32[]{:S(2)}, u32[]{:S(2)}) async-start(bf16[16,144,128]{2,1,0:T(8,128)(2,1)} %get-tuple-element.24), calls=%async_computation.1 | async-start | bytes 1179648 | tf_op jit(solution)/shard_map/all_to_all | solution.py:239
  32.1 20.4 %collective-permute-start.3 = (bf16[32,4096]{1,0:T(8,128)(2,1)}, bf16[32,4096]{1,0:T(8,128)(2,1)}, u32[]{:S(2)}, u32[]{:S(2)}) collective-permute-start(bf16[32,4096]{1,0:T(8,128)(2,1)} %get-tuple-element.28), channel_id=1, source_target_pairs={{0,64},{64,128},{128,192},{192,0},{1,65},{65,129},{129,193},{193,1... | collective-permute-start | bytes 786440 | tf_op jit(solution)/shard_map/ppermute | solution.py:244
  35.5 17.1 %collective-permute-start.4 = (bf16[32,4096]{1,0:T(8,128)(2,1)}, bf16[32,4096]{1,0:T(8,128)(2,1)}, u32[]{:S(2)}, u32[]{:S(2)}) collective-permute-start(bf16[32,4096]{1,0:T(8,128)(2,1)} %get-tuple-element.29), channel_id=1, source_target_pairs={{0,128},{64,192},{128,0},{192,64},{1,129},{65,193},{129,1},{193,65... | collective-permute-start | bytes 786440 | tf_op jit(solution)/shard_map/ppermute | solution.py:244
  40.1 12.5 %collective-permute-start.5 = (bf16[32,4096]{1,0:T(8,128)(2,1)}, bf16[32,4096]{1,0:T(8,128)(2,1)}, u32[]{:S(2)}, u32[]{:S(2)}) collective-permute-start(bf16[32,4096]{1,0:T(8,128)(2,1)} %get-tuple-element.30), channel_id=1, source_target_pairs={{0,192},{64,0},{128,64},{192,128},{1,193},{65,1},{129,65},{193,129... | collective-permute-start | bytes 786440 | tf_op jit(solution)/shard_map/ppermute | solution.py:244
  48.9 18.8 %collective-permute-start.1 = (bf16[16,144,128]{2,1,0:T(8,128)(2,1)S(1)}, bf16[16,144,128]{2,1,0:T(8,128)(2,1)S(1)}, u32[]{:S(2)}, u32[]{:S(2)}) collective-permute-start(bf16[16,144,128]{2,1,0:T(8,128)(2,1)S(1)} %all-to-all-done.1.near_ref), channel_id=1, source_target_pairs={{0,304},{16,32},{32,16},{48,256},{256,48},{272,288},{288,272},{304... | collective-permute-start | bytes 1769480 | tf_op jit(solution)/shard_map/ppermute | solution.py:241
  52.6 1.0 %copy-start.6 = (f32[32,4096]{1,0:T(8,128)S(1)}, f32[32,4096]{1,0:T(8,128)}, u32[]{:S(2)}) copy-start(f32[32,4096]{1,0:T(8,128)} %copy-done.5) | copy-start | bytes 1572868
  55.0 0.7 copy-start.4
  55.7 18.9 %all-to-all-start.2 = ((bf16[32,32,128]{2,1,0:T(8,128)(2,1)}), bf16[32,32,128]{2,1,0:T(8,128)(2,1)}, u32[]{:S(2)}, u32[]{:S(2)}) async-start(bf16[32,32,128]{2,1,0:T(8,128)(2,1)} %copy-done.4), calls=%async_computation.2 | async-start | bytes 524288 | tf_op jit(solution)/shard_map/all_to_all | solution.py:256
  67.7 1.6 %copy-start.2 = (bf16[256,4096]{1,0:T(8,128)(2,1)S(1)}, bf16[256,4096]{1,0:T(8,128)(2,1)}, u32[]{:S(2)}) copy-start(bf16[256,4096]{1,0:T(8,128)(2,1)} %copy-done) | copy-start | bytes 6291460
  71.2 14.7 %collective-permute-start.2 = (f32[256,128]{1,0:T(8,128)}, f32[256,128]{1,0:T(8,128)S(1)}, u32[]{:S(2)}, u32[]{:S(2)}) collective-permute-start(f32[256,128]{1,0:T(8,128)} %get-tuple-element.26), channel_id=1, source_target_pairs={{0,1},{1,0},{2,3},{3,2},{4,5},{5,4},{6,7},{7,6},{8,9},{9,8},{10,11... | collective-permute-start | bytes 393224 | tf_op jit(solution)/shard_map/ppermute | solution.py:265
  76.3 21.1 %all-to-all-start.3 = ((f32[8,40,128]{2,1,0:T(8,128)}), f32[8,40,128]{2,1,0:T(8,128)S(1)}, u32[]{:S(2)}, u32[]{:S(2)}) async-start(f32[8,40,128]{2,1,0:T(8,128)} %shard_map.99), calls=%async_computation.3 | async-start | bytes 327680 | tf_op jit(solution)/shard_map/all_to_all | solution.py:277
